TPU v7x, 32 devices: a whole 2x2x4 slice. The times are simulated.
32 devices in a mesh: gx: 16 (over z, x, core), gy: 2 (over y).
Axes of the slice: x: 2, y: 2, z: 4, core: 2. Of those that a mesh axis runs over, the one named last changes fastest.
Arguments:
- populations: float32 [19, 64, 64, 128], P(None, 'gx', 'gy'), may hold values from 0 to 1, as said below
- labels: int32 [64, 64, 128], P('gx', 'gy'), may hold values from 0 to 3
- solid_mask: int32 [64, 64, 128], P('gx', 'gy'), may hold values 0 or 1
Outputs:
- new_populations: float32 [19, 64, 64, 128], P(None, 'gx', 'gy')
- phase: float32 [64, 64, 128], P('gx', 'gy')
Inputs may be any that keep to these rules, and one draw needn't show every extreme that they name: `populations`: every entry is positive.
All inputs are finite; a program needn't handle non-finite values. No bound on the sum of `solid_mask` on one device may be relied on, other than what follows from the above.
Results may differ from a plain program's by a relative error of at most 0.00011.
Values sent between devices are 32-bit elements; how exact they have to be, the bound alone decides.
A program may use at most 64 MiB of HBM per device.

v0:
```python
import jax
import jax.numpy as jnp
import numpy as np
from jax import lax
from jax.sharding import PartitionSpec as P

STEPS = 2


VELOCITY_SET = [
    (0, 0, 0),
    (1, 0, 0),
    (-1, 0, 0),
    (0, 1, 0),
    (0, -1, 0),
    (0, 0, 1),
    (0, 0, -1),
    (1, 1, 0),
    (-1, -1, 0),
    (1, -1, 0),
    (-1, 1, 0),
    (1, 0, 1),
    (-1, 0, -1),
    (1, 0, -1),
    (-1, 0, 1),
    (0, 1, 1),
    (0, -1, -1),
    (0, 1, -1),
    (0, -1, 1),
]
OPPOSITE = [0, 2, 1, 4, 3, 6, 5, 8, 7, 10, 9, 12, 11, 14, 13, 16, 15, 18, 17]
WEIGHTS = [1.0 / 3.0] + [1.0 / 18.0] * 6 + [1.0 / 36.0] * 12
BALANCE = [-1.0 / 3.0] + [1.0 / 18.0] * 6 + [1.0 / 36.0] * 12
RELAX_RATES = [
    0.0,
    0.0,
    0.0,
    0.0,
    1.0,
    1.25,
    1.25,
    1.25,
    1.25,
    1.25,
    1.2,
    1.2,
    1.2,
    1.2,
    1.2,
    1.2,
    1.4,
    1.4,
    1.4,
]
SURFACE_COEF = 0.2
SEGREGATION_RATE = 0.7
GRAD_FLOOR = 0.1


def with_halo(block, sides, width):
    for axis, dim in sides:
        count = lax.axis_size(axis)
        forward = [(i, i + 1) for i in range(count - 1)]
        forward.append((count - 1, 0))
        backward = [(target, source) for source, target in forward]
        low = lax.ppermute(
            lax.slice_in_dim(block, block.shape[dim] - width, None, axis=dim), axis, forward
        )
        high = lax.ppermute(lax.slice_in_dim(block, 0, width, axis=dim), axis, backward)
        block = jnp.concatenate([low, block, high], axis=dim)
    return block


def moment_values(ex, ey, ez):
    return [
        1.0,
        ex,
        ey,
        ez,
        ex * ex + ey * ey + ez * ez,
        ex * ex - ey * ey,
        ey * ey - ez * ez,
        ex * ey,
        ex * ez,
        ey * ez,
        ex * ex * ey,
        ex * ex * ez,
        ey * ey * ex,
        ey * ey * ez,
        ez * ez * ex,
        ez * ez * ey,
        ex * ex * ey * ey,
        ex * ex * ez * ez,
        ey * ey * ez * ez,
    ]


def build_collision():
    count = 19
    columns = [moment_values(float(v[0]), float(v[1]), float(v[2])) for v in VELOCITY_SET]
    moments = [
        [columns[col_index][row_index] for col_index in range(count)] for row_index in range(count)
    ]
    augmented = [
        moments[row_index][:]
        + [1.0 if row_index == col_index else 0.0 for col_index in range(count)]
        for row_index in range(count)
    ]
    for column in range(count):
        pivot_row = column
        for row_index in range(column + 1, count):
            if abs(augmented[row_index][column]) > abs(augmented[pivot_row][column]):
                pivot_row = row_index
        augmented[column], augmented[pivot_row] = (augmented[pivot_row], augmented[column])
        leading = augmented[column][column]
        augmented[column] = [entry / leading for entry in augmented[column]]
        for row_index in range(count):
            if row_index != column:
                factor = augmented[row_index][column]
                if factor != 0.0:
                    augmented[row_index] = [
                        entry - factor * pivot_entry
                        for entry, pivot_entry in zip(augmented[row_index], augmented[column])
                    ]
    inverse = [augmented[row_index][count:] for row_index in range(count)]
    result = [
        [
            sum(
                (
                    inverse[row_index][inner] * RELAX_RATES[inner] * moments[inner][col_index]
                    for inner in range(count)
                )
            )
            for col_index in range(count)
        ]
        for row_index in range(count)
    ]
    return np.array(result, dtype=np.float32)


def velocity_table():
    return np.array(VELOCITY_SET, dtype=np.float32).T.copy()


def gradient_of(padded, size_x, size_y):
    shape = (size_x, size_y, padded.shape[2])
    grad_x = jnp.zeros(shape, jnp.float32)
    grad_y = jnp.zeros(shape, jnp.float32)
    grad_z = jnp.zeros(shape, jnp.float32)
    for direction in range(1, 19):
        ex, ey, ez = VELOCITY_SET[direction]
        part = padded[1 + ex : 1 + ex + size_x, 1 + ey : 1 + ey + size_y]
        value = jnp.roll(part, -ez, axis=2)
        factor = 3.0 * WEIGHTS[direction]
        if ex != 0:
            grad_x = grad_x + factor * ex * value
        if ey != 0:
            grad_y = grad_y + factor * ey * value
        if ez != 0:
            grad_z = grad_z + factor * ez * value
    return jnp.stack([grad_x, grad_y, grad_z])


def collide(pops, phase, grad, wall_nodes):
    tail = (1,) * (pops.ndim - 1)
    lattice_weights = jnp.asarray(WEIGHTS, jnp.float32).reshape((19,) + tail)
    balance = jnp.asarray(BALANCE, jnp.float32).reshape((19,) + tail)
    table = jnp.asarray(velocity_table(), jnp.float32)
    collision_k = jnp.asarray(build_collision(), jnp.float32)
    highest = lax.Precision.HIGHEST
    fluid_density = jnp.sum(pops, axis=0)
    momentum = jnp.einsum("ci,i...->c...", table, pops, precision=highest)
    velocity = momentum / fluid_density
    projected = jnp.einsum("ci,c...->i...", table, velocity, precision=highest)
    speed_sq = jnp.sum(velocity * velocity, axis=0)
    equilibrium = (
        lattice_weights
        * fluid_density
        * (1.0 + 3.0 * projected + 4.5 * projected * projected - 1.5 * speed_sq)
    )
    relaxed = pops - jnp.einsum("ij,j...->i...", collision_k, pops - equilibrium, precision=highest)
    grad_sq = jnp.sum(grad * grad, axis=0)
    clipped_values = jnp.maximum(jnp.sqrt(grad_sq), GRAD_FLOOR)
    aligned_component = jnp.einsum("ci,c...->i...", table, grad, precision=highest)
    surface_perturbation = (
        relaxed
        + 0.5
        * SURFACE_COEF
        * (lattice_weights * aligned_component * aligned_component - balance * grad_sq)
        / clipped_values
    )
    red_fraction = 0.5 * (1.0 + phase)
    separated_colours = (
        red_fraction * surface_perturbation
        + SEGREGATION_RATE
        * 0.25
        * fluid_density
        * (1.0 - phase * phase)
        * lattice_weights
        * aligned_component
        / clipped_values
    )
    reflected_populations = pops[np.array(OPPOSITE)]
    total_post = jnp.where(wall_nodes, reflected_populations, surface_perturbation)
    red_after_collide = jnp.where(
        wall_nodes, red_fraction * reflected_populations, separated_colours
    )
    return (total_post, red_after_collide)


def on_device(populations, labels, solid_mask):
    size_x, size_y, size_z = labels.shape
    y_count = lax.axis_size("gy")
    y_index = lax.axis_index("gy")
    ypos_global = y_index * size_y + jnp.arange(size_y)
    wall = (ypos_global == 0) | (ypos_global == size_y * y_count - 1)
    wall_nodes = (solid_mask > 0) | wall[None, :, None]
    ypad = jnp.arange(size_y + 2)
    outside = (ypad == 0) & (y_index == 0) | (ypad == size_y + 1) & (y_index == y_count - 1)
    rim_keep = jnp.where(outside, 0.0, 1.0).astype(jnp.float32)
    phase = jnp.where(labels > 0, 1.0, -1.0).astype(jnp.float32)
    pops = populations
    for step in range(STEPS):
        padded = with_halo(phase, (("gx", 0), ("gy", 1)), 1)
        padded = padded * rim_keep[None, :, None]
        grad = gradient_of(padded, size_x, size_y)
        total_post, red_after_collide = collide(pops, phase, grad, wall_nodes)
        stacked = jnp.concatenate([total_post, red_after_collide], axis=0)
        widened = with_halo(stacked, (("gx", 1), ("gy", 2)), 1)
        widened = widened * rim_keep[None, None, :, None]
        parts = []
        for component in range(38):
            ex, ey, ez = VELOCITY_SET[component % 19]
            piece = widened[component, 1 - ex : 1 - ex + size_x, 1 - ey : 1 - ey + size_y]
            parts.append(jnp.roll(piece, ez, axis=2))
        moved = jnp.stack(parts)
        pops = moved[:19]
        phase = 2.0 * jnp.sum(moved[19:], axis=0) / jnp.sum(pops, axis=0) - 1.0
    return (pops, phase)


def solution(mesh):
    in_specs = (P(None, "gx", "gy", None), P("gx", "gy", None), P("gx", "gy", None))
    out_specs = (P(None, "gx", "gy", None), P("gx", "gy", None))
    return jax.shard_map(
        on_device, mesh=mesh, in_specs=in_specs, out_specs=out_specs, check_vma=False
    )
```

profile of v0, /device:TPU:0, one launch (start us, length us, event | category | flops | bytes accessed | tf_op | source)
XLA Modules:
  0.0 102.2 jit_solution(7654955330817529247)
XLA Ops:
  0.7 1.5 %reduce_sum.465 = f32[4,32,128]{2,1,0:T(8,128)S(1)} reduce(f32[19,4,32,128]{3,2,1,0:T(8,128)} %param.15, f32[]{:T(128)} %constant.32.clone.1), dimensions={0}, to_apply=%region_0.1 | reduce | flops 294912 | bytes 1310724 | tf_op jit(solution)/shard_map/reduce_sum | solution.py:171
  2.7 5.0 %collective-permute-start.1 = (f32[1,32,128]{2,1,0:T(8,128)S(1)}, f32[1,32,128]{2,1,0:T(8,128)S(1)}, u32[]{:S(2)}, u32[]{:S(2)}) collective-permute-start(f32[1,32,128]{2,1,0:T(8,128)S(1)} %get-tuple-element.207), channel_id=1, source_target_pairs={{2,0},{4,2},{6,4},{8,6},{10,8},{12,10},{14,12},{16,14},{18,16},{20... | collective-permute-start | bytes 49160 | tf_op jit(solution)/shard_map/ppermute | solution.py:69
  7.8 1.7 %multiply_reduce_fusion.1 = (f32[4,32,128]{2,1,0:T(8,128)S(1)}, f32[3,4,32,128]{3,0,2,1:T(4,128)S(1)}) fusion(f32[4,32,128]{2,1,0:T(8,128)S(1)} %reduce_sum.465, f32[3,19,1,1]{1,0,3,2:T(4,128)S(1)} %copy-done.6, f32[19,4,32,128]{3,2,1,0:T(8,128)S(1)} %copy-done), kind=kOutput, calls=%fused_computation.58 | convolution fusion | flops 11337728 | bytes 1573092 | tf_op jit(solution)/shard_map/ci,i...->c.../dot_general | solution.py:172
  9.5 1.5 %fusion.200 = f32[19,4,32,128]{3,0,2,1:T(8,128)S(1)} fusion(f32[3,19,1,1]{1,0,3,2:T(4,128)S(1)} %copy-done.6, f32[3,4,32,128]{3,0,2,1:T(4,128)S(1)} %get-tuple-element.209), kind=kOutput, calls=%fused_computation.461 | convolution fusion | flops 11206656 | bytes 1442020 | tf_op jit(solution)/shard_map/ci,c...->i.../dot_general | solution.py:174
  11.9 4.1 %fusion.2 = f32[19,4,32,128]{3,0,2,1:T(8,128)S(1)} fusion(f32[19,19,1,1]{1,0,3,2:T(8,128)S(1)} %copy-done.5, f32[19,4,32,128]{3,2,1,0:T(8,128)S(1)} %copy-done, f32[19,4,32,128]{3,2,1,0:T(8,128)S(1)} %get-tuple-element.79, f32[19,4,32,128]{3,0,2,1:T(8,128)S(1)} %fusion.200, f32[19,4,32,128]{3,2,1,0:T(8,128)S(1)} %get-tuple-element.78, ...), kind=kOutput, calls=%fused_computation.10 | convolution fusion | flops 72843264 | bytes 6358512 | tf_op jit(solution)/shard_map/ij,j...->i.../dot_general | solution.py:181
  16.1 2.0 %collective-permute-start.2 = (f32[6,1,128]{2,1,0:T(1,128)S(1)}, f32[6,1,128]{2,1,0:T(1,128)S(1)}, u32[]{:S(2)}, u32[]{:S(2)}) collective-permute-start(f32[6,1,128]{2,1,0:T(1,128)S(1)} %get-tuple-element.159), channel_id=1, source_target_pairs={{0,1},{1,0},{2,3},{3,2},{4,5},{5,4},{6,7},{7,6},{8,9},{9,8},{10,11... | collective-permute-start | bytes 9224 | tf_op jit(solution)/shard_map/ppermute | solution.py:66
  18.2 1.7 %gather_fusion = f32[19,4,32,128]{3,2,1,0:T(8,128)} fusion(f32[19,4,32,128]{3,2,1,0:T(8,128)S(1)} %copy-done, s32[1024]{0:T(1024)S(1)} %pad_clamp_fusion), kind=kCustom, calls=%fused_computation | custom fusion | bytes 2490444 | tf_op jit(solution)/shard_map/gather | solution.py:203
  19.8 1.8 %collective-permute-done.3 = f32[6,1,128]{2,1,0:T(1,128)S(1)} collective-permute-done((f32[6,1,128]{2,1,0:T(1,128)S(1)}, f32[6,1,128]{2,1,0:T(1,128)S(1)}, u32[]{:S(2)}, u32[]{:S(2)}) %collective-permute-start.3) | collective-permute-done | bytes 3104 | tf_op jit(solution)/shard_map/ppermute | solution.py:69
  22.7 1.5 %fusion.37 = f32[19,4,32,128]{3,0,2,1:T(8,128)S(1)} fusion(f32[3,19,1,1]{1,0,3,2:T(4,128)S(1)} %copy-done.6, f32[3,4,32,128]{3,2,1,0:T(8,128)S(1)} %get-tuple-element.84), kind=kOutput, calls=%fused_computation.55 | convolution fusion | flops 11206656 | bytes 1442020 | tf_op jit(solution)/shard_map/ci,c...->i.../dot_general | solution.py:184
  25.3 4.4 %collective-permute-start.5 = (f32[38,1,32,128]{3,2,1,0:T(8,128)S(1)}, f32[38,1,32,128]{3,2,1,0:T(8,128)S(1)}, u32[]{:S(2)}, u32[]{:S(2)}) collective-permute-start(f32[38,1,32,128]{3,2,1,0:T(8,128)S(1)} %get-tuple-element.77), channel_id=1, source_target_pairs={{2,0},{4,2},{6,4},{8,6},{10,8},{12,10},{14,12},{16,14},{18,16},{20... | collective-permute-start | bytes 1867784 | tf_op jit(solution)/shard_map/ppermute | solution.py:69
  29.8 8.0 %collective-permute-done.4 = f32[38,1,32,128]{3,2,1,0:T(8,128)S(1)} collective-permute-done((f32[38,1,32,128]{3,2,1,0:T(8,128)S(1)}, f32[38,1,32,128]{3,2,1,0:T(8,128)S(1)}, u32[]{:S(2)}, u32[]{:S(2)}) %collective-permute-start.4) | collective-permute-done | bytes 622624 | tf_op jit(solution)/shard_map/ppermute | solution.py:66
  38.1 1.9 %collective-permute-start.7 = (f32[38,6,1,128]{3,2,1,0:T(1,128)S(1)}, f32[38,6,1,128]{3,2,1,0:T(1,128)S(1)}, u32[]{:S(2)}, u32[]{:S(2)}) collective-permute-start(f32[38,6,1,128]{3,2,1,0:T(1,128)S(1)} %get-tuple-element.73), channel_id=1, source_target_pairs={{1,0},{0,1},{3,2},{2,3},{5,4},{4,5},{7,6},{6,7},{9,8},{8,9},{11,10... | collective-permute-start | bytes 350216 | tf_op jit(solution)/shard_map/ppermute | solution.py:69
  40.0 2.8 %collective-permute-done.6 = f32[38,6,1,128]{3,2,1,0:T(1,128)S(1)} collective-permute-done((f32[38,6,1,128]{3,2,1,0:T(1,128)S(1)}, f32[38,6,1,128]{3,2,1,0:T(1,128)S(1)}, u32[]{:S(2)}, u32[]{:S(2)}) %collective-permute-start.6) | collective-permute-done | bytes 116768 | tf_op jit(solution)/shard_map/ppermute | solution.py:66
  42.8 1.9 %collective-permute-done.7 = f32[38,6,1,128]{3,2,1,0:T(1,128)S(1)} collective-permute-done((f32[38,6,1,128]{3,2,1,0:T(1,128)S(1)}, f32[38,6,1,128]{3,2,1,0:T(1,128)S(1)}, u32[]{:S(2)}, u32[]{:S(2)}) %collective-permute-start.7) | collective-permute-done | bytes 116768 | tf_op jit(solution)/shard_map/ppermute | solution.py:69
  44.7 2.0 %maximum_multiply_fusion = f32[38,6,34,128]{3,2,1,0:T(8,128)S(1)} fusion(f32[38,6,1,128]{3,2,1,0:T(1,128)S(1)} %collective-permute-done.7, f32[38,1,32,128]{3,2,1,0:T(8,128)S(1)} %collective-permute-done.5, f32[19,4,32,128]{3,2,1,0:T(8,128)S(1)} %get-tuple-element.10, f32[19,4,32,128]{3,2,1,0:T(8,128)S(1)} %get-tuple-element.9, ...), kind=kLoop, calls=%fused_computation.2 | loop fusion | flops 5953536 | bytes 7938184 | tf_op jit(solution)/shard_map/mul | solution.py:230
  50.6 1.7 %collective-permute-start.8 = (f32[1,32,128]{2,1,0:T(8,128)S(1)}, f32[1,32,128]{2,1,0:T(8,128)S(1)}, u32[]{:S(2)}, u32[]{:S(2)}) collective-permute-start(f32[1,32,128]{2,1,0:T(8,128)S(1)} %get-tuple-element.161), channel_id=1, source_target_pairs={{0,2},{2,4},{4,6},{6,8},{8,10},{10,12},{12,14},{14,16},{16,18},{18... | collective-permute-start | bytes 49160 | tf_op jit(solution)/shard_map/ppermute | solution.py:66
  52.4 2.8 %collective-permute-start.9 = (f32[1,32,128]{2,1,0:T(8,128)S(1)}, f32[1,32,128]{2,1,0:T(8,128)S(1)}, u32[]{:S(2)}, u32[]{:S(2)}) collective-permute-start(f32[1,32,128]{2,1,0:T(8,128)S(1)} %get-tuple-element.162), channel_id=1, source_target_pairs={{2,0},{4,2},{6,4},{8,6},{10,8},{12,10},{14,12},{16,14},{18,16},{20... | collective-permute-start | bytes 49160 | tf_op jit(solution)/shard_map/ppermute | solution.py:69
  55.1 1.9 %multiply_reduce_fusion = (f32[4,32,128]{2,1,0:T(8,128)S(1)}, f32[3,4,32,128]{3,0,2,1:T(4,128)S(1)}) fusion(f32[4,32,128]{2,1,0:T(8,128)S(1)} %bitcast.601, f32[3,19,1,1]{1,0,3,2:T(4,128)S(1)} %copy-done.6, f32[19,4,32,128]{3,2,1,0:T(8,128)S(1)} %constant_dynamic-update-slice_fusion), kind=kOutput, calls=%fused_computation.57 | convolution fusion | flops 11337728 | bytes 1573092 | tf_op jit(solution)/shard_map/ci,i...->c.../dot_general | solution.py:172
  57.1 1.5 %fusion.201 = f32[19,4,32,128]{3,0,2,1:T(8,128)S(1)} fusion(f32[3,19,1,1]{1,0,3,2:T(4,128)S(1)} %copy-done.6, f32[3,4,32,128]{3,0,2,1:T(4,128)S(1)} %get-tuple-element.211), kind=kOutput, calls=%fused_computation.462 | convolution fusion | flops 11206656 | bytes 1442020 | tf_op jit(solution)/shard_map/ci,c...->i.../dot_general | solution.py:174
  59.0 2.0 %fusion.3 = f32[19,4,32,128]{3,0,2,1:T(8,128)S(1)} fusion(f32[19,19,1,1]{1,0,3,2:T(8,128)S(1)} %copy-done.5, f32[19,4,32,128]{3,2,1,0:T(8,128)S(1)} %fusion.18), kind=kOutput, calls=%fused_computation.13 | convolution fusion | flops 70975488 | bytes 2491812 | tf_op jit(solution)/shard_map/ij,j...->i.../dot_general | solution.py:181
  61.0 1.2 %collective-permute-start.10 = (f32[6,1,128]{2,1,0:T(1,128)S(1)}, f32[6,1,128]{2,1,0:T(1,128)S(1)}, u32[]{:S(2)}, u32[]{:S(2)}) collective-permute-start(f32[6,1,128]{2,1,0:T(1,128)S(1)} %get-tuple-element.157), channel_id=1, source_target_pairs={{0,1},{1,0},{2,3},{3,2},{4,5},{5,4},{6,7},{7,6},{8,9},{9,8},{10,11... | collective-permute-start | bytes 9224 | tf_op jit(solution)/shard_map/ppermute | solution.py:66
  63.1 1.7 %gather_fusion.1 = f32[19,4,32,128]{3,2,1,0:T(8,128)} fusion(f32[19,4,32,128]{3,2,1,0:T(8,128)S(1)} %constant_dynamic-update-slice_fusion, s32[1024]{0:T(1024)S(1)} %pad_clamp_fusion), kind=kCustom, calls=%fused_computation.1 | custom fusion | bytes 2490444 | tf_op jit(solution)/shard_map/gather | solution.py:203
  66.9 1.5 %fusion.35 = f32[19,4,32,128]{3,0,2,1:T(8,128)S(1)} fusion(f32[3,19,1,1]{1,0,3,2:T(4,128)S(1)} %copy-done.6, f32[3,4,32,128]{3,2,1,0:T(8,128)S(1)} %get-tuple-element.81), kind=kOutput, calls=%fused_computation.53 | convolution fusion | flops 11206656 | bytes 1442020 | tf_op jit(solution)/shard_map/ci,c...->i.../dot_general | solution.py:184
  70.1 2.7 %copy_select_fusion = f32[19,4,32,128]{3,0,2,1:T(8,128)S(1)} fusion(f32[19,4,32,128]{3,2,1,0:T(8,128)S(1)} %get-tuple-element.80, f32[19,4,32,128]{3,2,1,0:T(8,128)S(1)} %broadcast_multiply_fusion, f32[19,4,32,128]{3,0,2,1:T(8,128)S(1)} %fusion.35, f32[4,32,128]{2,1,0:T(8,128)S(1)} %sqrt_maximum_fusion, f32[4,32,128]{2,1,0:T(8,128)S(1)} %get-tuple-element.4, ...), kind=kLoop, calls=%fused_computation.11 | loop fusion | flops 1556480 | bytes 5128268 | tf_op jit(solution)/shard_map/jit(_where)/select_n | solution.py:205
  73.8 7.1 %collective-permute-done.13 = f32[38,1,32,128]{3,2,1,0:T(8,128)S(1)} collective-permute-done((f32[38,1,32,128]{3,2,1,0:T(8,128)S(1)}, f32[38,1,32,128]{3,2,1,0:T(8,128)S(1)}, u32[]{:S(2)}, u32[]{:S(2)}) %collective-permute-start.13) | collective-permute-done | bytes 622624 | tf_op jit(solution)/shard_map/ppermute | solution.py:69
  81.2 4.5 %collective-permute-done.12 = f32[38,1,32,128]{3,2,1,0:T(8,128)S(1)} collective-permute-done((f32[38,1,32,128]{3,2,1,0:T(8,128)S(1)}, f32[38,1,32,128]{3,2,1,0:T(8,128)S(1)}, u32[]{:S(2)}, u32[]{:S(2)}) %collective-permute-start.12) | collective-permute-done | bytes 622624 | tf_op jit(solution)/shard_map/ppermute | solution.py:66
  87.2 1.1 %collective-permute-start.15 = (f32[38,6,1,128]{3,0,2,1:T(8,128)S(1)}, f32[38,6,1,128]{3,0,2,1:T(8,128)S(1)}, u32[]{:S(2)}, u32[]{:S(2)}) collective-permute-start(f32[38,6,1,128]{3,0,2,1:T(8,128)S(1)} %get-tuple-element.33), channel_id=1, source_target_pairs={{1,0},{0,1},{3,2},{2,3},{5,4},{4,5},{7,6},{6,7},{9,8},{8,9},{11,10... | collective-permute-start | bytes 350216 | tf_op jit(solution)/shard_map/ppermute | solution.py:69
  88.3 3.8 %collective-permute-done.14 = f32[38,6,1,128]{3,0,2,1:T(8,128)S(1)} collective-permute-done((f32[38,6,1,128]{3,0,2,1:T(8,128)S(1)}, f32[38,6,1,128]{3,0,2,1:T(8,128)S(1)}, u32[]{:S(2)}, u32[]{:S(2)}) %collective-permute-start.14) | collective-permute-done | bytes 116768 | tf_op jit(solution)/shard_map/ppermute | solution.py:66
  92.1 2.6 %collective-permute-done.15 = f32[38,6,1,128]{3,0,2,1:T(8,128)S(1)} collective-permute-done((f32[38,6,1,128]{3,0,2,1:T(8,128)S(1)}, f32[38,6,1,128]{3,0,2,1:T(8,128)S(1)}, u32[]{:S(2)}, u32[]{:S(2)}) %collective-permute-start.15) | collective-permute-done | bytes 116768 | tf_op jit(solution)/shard_map/ppermute | solution.py:69
  95.6 1.3 %fusion.172 = (f32[1,4,32,128]{3,0,2,1:T(1,128)S(1)}, f32[1,4,32,128]{3,0,2,1:T(1,128)S(1)}, f32[1,4,32,128]{3,0,2,1:T(1,128)S(1)}, f32[1,4,32,128]{3,0,2,1:T(1,...) fusion(f32[38,6,34,128]{3,0,2,1:T(8,128)S(1)} %maximum_multiply, ...), kind=kLoop, calls=%fused_computation.433 | loop fusion | bytes 2490368 | tf_op jit(solution)/shard_map/slice | solution.py:234
  96.9 1.2 %fusion.173 = (f32[1,4,32,128]{3,0,2,1:T(1,128)S(1)}, f32[1,4,32,128]{3,0,2,1:T(1,128)S(1)}, f32[1,4,32,128]{3,0,2,1:T(1,128)S(1)}, f32[1,4,32,128]{3,0,2,1:T(1,...) fusion(f32[38,6,34,128]{3,0,2,1:T(8,128)S(1)} %maximum_multiply, ...), kind=kLoop, calls=%fused_computation.434 | loop fusion | bytes 2490368 | tf_op jit(solution)/shard_map/slice | solution.py:234
  100.9 1.2 %fusion.169 = f32[4,32,128]{2,1,0:T(8,128)} fusion(f32[4,32,128]{2,1,0:T(8,128)S(1)} %bitcast.582, f32[4,32,128]{2,1,0:T(8,128)S(1)} %bitcast.584, f32[4,32,128]{2,1,0:T(8,128)S(1)} %bitcast.586, f32[4,32,128]{2,1,0:T(8,128)S(1)} %bitcast.588, f32[1,4,32,128]{3,2,1,0:T(8,128)S(1)} %bitcast.590, f32[1,4,32,128]{3,2,1,0:T(8,128)S(1)} %bitcast.592, ...), kind=kLoop, calls=%fused_computation.369 | loop fusion | flops 966656 | bytes 2555904 | tf_op jit(solution)/shard_map/sub | solution.py:238
  (162 shorter events, 19.1 us)
Async XLA Ops:
  0.6 7.1 %copy-start.6 = (f32[3,19,1,1]{1,0,3,2:T(4,128)S(1)}, f32[3,19,1,1]{1,0,3,2:T(4,128)}, u32[]{:S(2)}) copy-start(f32[3,19,1,1]{1,0,3,2:T(4,128)} %constant.78) | copy-start | bytes 688
  0.6 7.1 %copy-start = (f32[19,4,32,128]{3,2,1,0:T(8,128)S(1)}, f32[19,4,32,128]{3,2,1,0:T(8,128)}, u32[]{:S(2)}) copy-start(f32[19,4,32,128]{3,2,1,0:T(8,128)} %param.15) | copy-start | bytes 3735556
  0.7 1.5 %copy-start.3 = (s32[4,32,128]{2,1,0:T(8,128)S(1)}, s32[4,32,128]{2,1,0:T(8,128)}, u32[]{:S(2)}) copy-start(s32[4,32,128]{2,1,0:T(8,128)} %param.16) | copy-start | bytes 196612
  2.2 13.8 %collective-permute-start = (f32[1,32,128]{2,1,0:T(8,128)S(1)}, f32[1,32,128]{2,1,0:T(8,128)S(1)}, u32[]{:S(2)}, u32[]{:S(2)}) collective-permute-start(f32[1,32,128]{2,1,0:T(8,128)S(1)} %get-tuple-element.206), channel_id=1, source_target_pairs={{0,2},{2,4},{4,6},{6,8},{8,10},{10,12},{12,14},{14,16},{16,18},{18... | collective-permute-start | bytes 49160 | tf_op jit(solution)/shard_map/ppermute | solution.py:66
  2.7 13.3 %collective-permute-start.1 = (f32[1,32,128]{2,1,0:T(8,128)S(1)}, f32[1,32,128]{2,1,0:T(8,128)S(1)}, u32[]{:S(2)}, u32[]{:S(2)}) collective-permute-start(f32[1,32,128]{2,1,0:T(8,128)S(1)} %get-tuple-element.207), channel_id=1, source_target_pairs={{2,0},{4,2},{6,4},{8,6},{10,8},{12,10},{14,12},{16,14},{18,16},{20... | collective-permute-start | bytes 49160 | tf_op jit(solution)/shard_map/ppermute | solution.py:69
  11.0 0.8 copy-start.4
  11.0 0.9 copy-start.5
  11.0 0.9 copy-start.7
  11.9 4.1 %copy-start.10 = (s32[19]{0:T(128)S(1)}, s32[19]{0:T(128)}, u32[]{:S(2)}) copy-start(s32[19]{0:T(128)} %constant.75) | copy-start | bytes 232
  16.1 3.8 %collective-permute-start.2 = (f32[6,1,128]{2,1,0:T(1,128)S(1)}, f32[6,1,128]{2,1,0:T(1,128)S(1)}, u32[]{:S(2)}, u32[]{:S(2)}) collective-permute-start(f32[6,1,128]{2,1,0:T(1,128)S(1)} %get-tuple-element.159), channel_id=1, source_target_pairs={{0,1},{1,0},{2,3},{3,2},{4,5},{5,4},{6,7},{7,6},{8,9},{9,8},{10,11... | collective-permute-start | bytes 9224 | tf_op jit(solution)/shard_map/ppermute | solution.py:66
  18.1 3.6 %collective-permute-start.3 = (f32[6,1,128]{2,1,0:T(1,128)S(1)}, f32[6,1,128]{2,1,0:T(1,128)S(1)}, u32[]{:S(2)}, u32[]{:S(2)}) collective-permute-start(f32[6,1,128]{2,1,0:T(1,128)S(1)} %get-tuple-element.160), channel_id=1, source_target_pairs={{1,0},{0,1},{3,2},{2,3},{5,4},{4,5},{7,6},{6,7},{9,8},{8,9},{11,10... | collective-permute-start | bytes 9224 | tf_op jit(solution)/shard_map/ppermute | solution.py:69
  22.7 1.6 %copy-start.2 = (f32[19,4,32,128]{3,2,1,0:T(8,128)S(1)}, f32[19,4,32,128]{3,2,1,0:T(8,128)}, u32[]{:S(2)}) copy-start(f32[19,4,32,128]{3,2,1,0:T(8,128)} %gather_fusion) | copy-start | bytes 3735556
  22.7 1.6 %copy-start.9 = (f32[19]{0:T(128)S(1)}, f32[19]{0:T(128)}, u32[]{:S(2)}) copy-start(f32[19]{0:T(128)} %constant.25.clone) | copy-start | bytes 232
  25.3 12.5 %collective-permute-start.4 = (f32[38,1,32,128]{3,2,1,0:T(8,128)S(1)}, f32[38,1,32,128]{3,2,1,0:T(8,128)S(1)}, u32[]{:S(2)}, u32[]{:S(2)}) collective-permute-start(f32[38,1,32,128]{3,2,1,0:T(8,128)S(1)} %get-tuple-element.76), channel_id=1, source_target_pairs={{0,2},{2,4},{4,6},{6,8},{8,10},{10,12},{12,14},{14,16},{16,18},{18... | collective-permute-start | bytes 1867784 | tf_op jit(solution)/shard_map/ppermute | solution.py:66
  25.3 12.5 %collective-permute-start.5 = (f32[38,1,32,128]{3,2,1,0:T(8,128)S(1)}, f32[38,1,32,128]{3,2,1,0:T(8,128)S(1)}, u32[]{:S(2)}, u32[]{:S(2)}) collective-permute-start(f32[38,1,32,128]{3,2,1,0:T(8,128)S(1)} %get-tuple-element.77), channel_id=1, source_target_pairs={{2,0},{4,2},{6,4},{8,6},{10,8},{12,10},{14,12},{16,14},{18,16},{20... | collective-permute-start | bytes 1867784 | tf_op jit(solution)/shard_map/ppermute | solution.py:69
  37.9 4.9 %collective-permute-start.6 = (f32[38,6,1,128]{3,2,1,0:T(1,128)S(1)}, f32[38,6,1,128]{3,2,1,0:T(1,128)S(1)}, u32[]{:S(2)}, u32[]{:S(2)}) collective-permute-start(f32[38,6,1,128]{3,2,1,0:T(1,128)S(1)} %get-tuple-element.72), channel_id=1, source_target_pairs={{0,1},{1,0},{2,3},{3,2},{4,5},{5,4},{6,7},{7,6},{8,9},{9,8},{10,11... | collective-permute-start | bytes 350216 | tf_op jit(solution)/shard_map/ppermute | solution.py:66
  38.1 6.6 %collective-permute-start.7 = (f32[38,6,1,128]{3,2,1,0:T(1,128)S(1)}, f32[38,6,1,128]{3,2,1,0:T(1,128)S(1)}, u32[]{:S(2)}, u32[]{:S(2)}) collective-permute-start(f32[38,6,1,128]{3,2,1,0:T(1,128)S(1)} %get-tuple-element.73), channel_id=1, source_target_pairs={{1,0},{0,1},{3,2},{2,3},{5,4},{4,5},{7,6},{6,7},{9,8},{8,9},{11,10... | collective-permute-start | bytes 350216 | tf_op jit(solution)/shard_map/ppermute | solution.py:69
  50.6 10.3 %collective-permute-start.8 = (f32[1,32,128]{2,1,0:T(8,128)S(1)}, f32[1,32,128]{2,1,0:T(8,128)S(1)}, u32[]{:S(2)}, u32[]{:S(2)}) collective-permute-start(f32[1,32,128]{2,1,0:T(8,128)S(1)} %get-tuple-element.161), channel_id=1, source_target_pairs={{0,2},{2,4},{4,6},{6,8},{8,10},{10,12},{12,14},{14,16},{16,18},{18... | collective-permute-start | bytes 49160 | tf_op jit(solution)/shard_map/ppermute | solution.py:66
  52.4 8.6 %collective-permute-start.9 = (f32[1,32,128]{2,1,0:T(8,128)S(1)}, f32[1,32,128]{2,1,0:T(8,128)S(1)}, u32[]{:S(2)}, u32[]{:S(2)}) collective-permute-start(f32[1,32,128]{2,1,0:T(8,128)S(1)} %get-tuple-element.162), channel_id=1, source_target_pairs={{2,0},{4,2},{6,4},{8,6},{10,8},{12,10},{14,12},{16,14},{18,16},{20... | collective-permute-start | bytes 49160 | tf_op jit(solution)/shard_map/ppermute | solution.py:69
  61.0 3.8 %collective-permute-start.10 = (f32[6,1,128]{2,1,0:T(1,128)S(1)}, f32[6,1,128]{2,1,0:T(1,128)S(1)}, u32[]{:S(2)}, u32[]{:S(2)}) collective-permute-start(f32[6,1,128]{2,1,0:T(1,128)S(1)} %get-tuple-element.157), channel_id=1, source_target_pairs={{0,1},{1,0},{2,3},{3,2},{4,5},{5,4},{6,7},{7,6},{8,9},{9,8},{10,11... | collective-permute-start | bytes 9224 | tf_op jit(solution)/shard_map/ppermute | solution.py:66
  62.2 3.6 %collective-permute-start.11 = (f32[6,1,128]{2,1,0:T(1,128)S(1)}, f32[6,1,128]{2,1,0:T(1,128)S(1)}, u32[]{:S(2)}, u32[]{:S(2)}) collective-permute-start(f32[6,1,128]{2,1,0:T(1,128)S(1)} %get-tuple-element.158), channel_id=1, source_target_pairs={{1,0},{0,1},{3,2},{2,3},{5,4},{4,5},{7,6},{6,7},{9,8},{8,9},{11,10... | collective-permute-start | bytes 9224 | tf_op jit(solution)/shard_map/ppermute | solution.py:69
  66.8 1.6 %copy-start.1 = (f32[19,4,32,128]{3,2,1,0:T(8,128)S(1)}, f32[19,4,32,128]{3,2,1,0:T(8,128)}, u32[]{:S(2)}) copy-start(f32[19,4,32,128]{3,2,1,0:T(8,128)} %gather_fusion.1) | copy-start | bytes 3735556
  73.1 7.8 %collective-permute-start.13 = (f32[38,1,32,128]{3,2,1,0:T(8,128)S(1)}, f32[38,1,32,128]{3,2,1,0:T(8,128)S(1)}, u32[]{:S(2)}, u32[]{:S(2)}) collective-permute-start(f32[38,1,32,128]{3,2,1,0:T(8,128)S(1)} %copy.271), channel_id=1, source_target_pairs={{2,0},{4,2},{6,4},{8,6},{10,8},{12,10},{14,12},{16,14},{18,16},{20... | collective-permute-start | bytes 1867784 | tf_op jit(solution)/shard_map/ppermute | solution.py:69
  73.3 12.5 %collective-permute-start.12 = (f32[38,1,32,128]{3,2,1,0:T(8,128)S(1)}, f32[38,1,32,128]{3,2,1,0:T(8,128)S(1)}, u32[]{:S(2)}, u32[]{:S(2)}) collective-permute-start(f32[38,1,32,128]{3,2,1,0:T(8,128)S(1)} %copy.270), channel_id=1, source_target_pairs={{0,2},{2,4},{4,6},{6,8},{8,10},{10,12},{12,14},{14,16},{16,18},{18... | collective-permute-start | bytes 1867784 | tf_op jit(solution)/shard_map/ppermute | solution.py:66
  86.2 5.9 %collective-permute-start.14 = (f32[38,6,1,128]{3,0,2,1:T(8,128)S(1)}, f32[38,6,1,128]{3,0,2,1:T(8,128)S(1)}, u32[]{:S(2)}, u32[]{:S(2)}) collective-permute-start(f32[38,6,1,128]{3,0,2,1:T(8,128)S(1)} %get-tuple-element.32), channel_id=1, source_target_pairs={{0,1},{1,0},{2,3},{3,2},{4,5},{5,4},{6,7},{7,6},{8,9},{9,8},{10,11... | collective-permute-start | bytes 350216 | tf_op jit(solution)/shard_map/ppermute | solution.py:66
  87.2 7.5 %collective-permute-start.15 = (f32[38,6,1,128]{3,0,2,1:T(8,128)S(1)}, f32[38,6,1,128]{3,0,2,1:T(8,128)S(1)}, u32[]{:S(2)}, u32[]{:S(2)}) collective-permute-start(f32[38,6,1,128]{3,0,2,1:T(8,128)S(1)} %get-tuple-element.33), channel_id=1, source_target_pairs={{1,0},{0,1},{3,2},{2,3},{5,4},{4,5},{7,6},{6,7},{9,8},{8,9},{11,10... | collective-permute-start | bytes 350216 | tf_op jit(solution)/shard_map/ppermute | solution.py:69
  100.9 1.2 %copy-start.8 = (f32[19,4,32,128]{3,2,1,0:T(8,128)}, f32[19,4,32,128]{3,2,1,0:T(8,128)S(1)}, u32[]{:S(2)}) copy-start(f32[19,4,32,128]{3,2,1,0:T(8,128)S(1)} %constant_dynamic-update-slice_fusion.19) | copy-start | bytes 3735556
where the time goes:
time: 102 us
  waiting for transfers between devices  33.6 us (33%)
  starting transfers between devices  23.5 us (23%)
  other arithmetic  15.6 us (15%)
  matrix products  15.5 us (15%)
  local copies, waits for them, and re-layouts  12.4 us (12%)
  between operations  1.58 us (2%)
    ppermute x8, waiting for transfers between devices, with_halo(): lax.ppermute(lax.slice_in_dim(block, block.shape[dim] - width, None, axis...  19.1 us
    ppermute x8, starting transfers between devices, with_halo(): lax.ppermute(lax.slice_in_dim(block, 0, width, axis=dim), axis, backward)  16.3 us
    ppermute x8, waiting for transfers between devices, with_halo(): lax.ppermute(lax.slice_in_dim(block, 0, width, axis=dim), axis, backward)  14.4 us
    ppermute x8, starting transfers between devices, with_halo(): lax.ppermute(lax.slice_in_dim(block, block.shape[dim] - width, None, axis...  7.19 us
    dot_general x2, matrix products, collide(): jnp.einsum('ij,j...->i...', collision_k, pops - equilibrium, precision=hi...  6.02 us
    dot_general x2, matrix products, collide(): momentum = jnp.einsum('ci,i...->c...', table, pops, precision=highest)  3.61 us
    slice x40, local copies, waits for them, and re-layouts, on_device(): parts.append(jnp.roll(piece, ez, axis=2))  3.4 us
    gather x2, local copies, waits for them, and re-layouts, collide(): reflected_populations = pops[np.array(OPPOSITE)]  3.32 us
  transfers between devices with their start and end apart: 16, of which 9 were waited for; matrix products, arithmetic and copies ran while one was open for 17% of the time, Pallas kernels for 0%

commit v1 on v0

v1 whole, which is shorter than its diff:
```python
import functools

import jax
import jax.numpy as jnp
from jax import lax
from jax.experimental import pallas as pl
from jax.experimental.pallas import tpu as pltpu
from jax.sharding import PartitionSpec as P

E = [
    (0, 0, 0), (1, 0, 0), (-1, 0, 0), (0, 1, 0), (0, -1, 0), (0, 0, 1), (0, 0, -1),
    (1, 1, 0), (-1, -1, 0), (1, -1, 0), (-1, 1, 0), (1, 0, 1), (-1, 0, -1), (1, 0, -1),
    (-1, 0, 1), (0, 1, 1), (0, -1, -1), (0, 1, -1), (0, -1, 1),
]
OPP = [0, 2, 1, 4, 3, 6, 5, 8, 7, 10, 9, 12, 11, 14, 13, 16, 15, 18, 17]
ORDER = [
    9, (1, -1), 1, 11, 13, (1, 0), 7, (1, 1),
    3, 15, 17, (0, 1), 10, (-1, 1),
    2, 12, 14, (-1, 0), 8, (-1, -1),
    4, 16, 18, (0, -1),
    0, 5, 6, (0, 0),
]
SLOT = {key: place for place, key in enumerate(ORDER)}
RED = [key for key in ORDER if isinstance(key, tuple)]
NS = len(ORDER)
PAD = 8
MESH = pl.DeviceIdType.MESH


def relax(f):
    def plane(pp, mm, pm, mp):
        s1, d1, s2, d2 = f[pp] + f[mm], f[pp] - f[mm], f[pm] + f[mp], f[pm] - f[mp]
        return s1 + s2, s1 - s2, d1 + d2, d1 - d2

    xy = plane(7, 8, 9, 10)
    xz = plane(11, 12, 13, 14)
    yz = plane(15, 16, 17, 18)
    sx, sy, sz = f[1] + f[2], f[3] + f[4], f[5] + f[6]
    rho = (f[0] + sx) + (sy + sz) + ((xy[0] + xz[0]) + yz[0])
    jx = (f[1] - f[2]) + (xy[2] + xz[2])
    jy = (f[3] - f[4]) + (xy[3] + yz[2])
    jz = (f[5] - f[6]) + (xz[3] + yz[3])
    inv = 1.0 / rho
    ux, uy, uz = jx * inv, jy * inv, jz * inv
    qx, qy, qz = jx * ux, jy * uy, jz * uz
    third = rho * (1.0 / 3.0)
    dxx = (sx + (xy[0] + xz[0])) - (third + qx)
    dyy = (sy + (xy[0] + yz[0])) - (third + qy)
    dzz = (sz + (xz[0] + yz[0])) - (third + qz)
    trace = (dxx + dyy) + dzz
    part = trace * (1.0 / 12.0)
    base = (third + ((qx + qy) + qz)) * (1.0 / 3.0)
    base = rho * (1.0 / 9.0) + ((qx + qy) + qz) * (1.0 / 3.0)
    tx, ty, tz = jx * (1.0 / 3.0), jy * (1.0 / 3.0), jz * (1.0 / 3.0)
    out = list(f)

    def edges(moments, rest, cross, ta, tb, pp, mm, pm, mp):
        four = (moments[0] - base) + 0.5 * rest
        a = 0.35 * four
        d = 0.3125 * (moments[1] - cross)
        b = 0.3 * (moments[2] - ta)
        c = 0.3 * (moments[3] - tb)
        p1, p2, q1, q2 = a + d, a - d, b + c, b - c
        out[pp] = f[pp] - (p1 + q1)
        out[mm] = f[mm] - (p1 - q1)
        out[pm] = f[pm] - (p2 + q2)
        out[mp] = f[mp] - (p2 - q2)
        return a, b, c

    axy, bxy, cxy = edges(xy, qz, jx * uy, tx, ty, 7, 8, 9, 10)
    axz, bxz, cxz = edges(xz, qy, jx * uz, tx, tz, 11, 12, 13, 14)
    ayz, byz, cyz = edges(yz, qx, jy * uz, ty, tz, 15, 16, 17, 18)

    def faces(delta, a, b, plus, minus):
        half = (0.625 * delta - 0.5 * part) - 2.0 * a
        diff = 2.0 * b
        out[plus] = f[plus] - (half - diff)
        out[minus] = f[minus] - (half + diff)

    faces(dxx, axy + axz, bxy + bxz, 1, 2)
    faces(dyy, axy + ayz, cxy + byz, 3, 4)
    faces(dzz, axz + ayz, cxz + cyz, 5, 6)
    out[0] = f[0] + (trace - 4.0 * ((axy + axz) + ayz))
    return out, rho


def kernel(nx, ny, pops_ref, labels_ref, mask_ref, out_ref, phase_ref,
           f0, f1, p0, p1, rho_ref, send_sem, recv_sem):
    lx, ly, lz = labels_ref.shape
    rt = ly // 8
    top = PAD + ly
    gx, gy = lax.axis_index("gx"), lax.axis_index("gy")
    xp, xm = lax.rem(gx + 1, nx), lax.rem(gx + nx - 1, nx)
    up, down = gy < ny - 1, gy > 0

    barrier = pltpu.get_barrier_semaphore()

    def greet(ax, ay):
        pl.semaphore_signal(barrier, inc=1, device_id=(ax, ay), device_id_type=MESH)

    greet(xp, gy)
    greet(xm, gy)
    for flag, ay in ((up, gy + 1), (down, gy - 1)):
        @pl.when(flag)
        def _():
            greet(gx, ay)
            greet(xp, ay)
            greet(xm, ay)

    def move(ref, src, dst, k, ax, ay):
        return pltpu.make_async_remote_copy(
            src_ref=ref.at[src], dst_ref=ref.at[dst],
            send_sem=send_sem.at[k], recv_sem=recv_sem.at[k],
            device_id=(ax, ay), device_id_type=MESH)

    mid = pl.ds(PAD, ly)
    last, ghost_low = pl.ds(top - 8, 8), pl.ds(0, 8)
    first, ghost_high = pl.ds(PAD, 8), pl.ds(top, 8)
    own = pl.ds(1, lx)

    def phase_messages(ref, k):
        return [
            ("x", move(ref, (lx, mid), (0, mid), k, xp, gy), None, None),
            ("x", move(ref, (1, mid), (lx + 1, mid), k + 1, xm, gy), None, None),
            ("y", move(ref, (own, last), (own, ghost_low), k + 2, gx, gy + 1), up, down),
            ("y", move(ref, (own, first), (own, ghost_high), k + 3, gx, gy - 1), down, up),
            ("x", move(ref, (lx, last), (0, ghost_low), k + 4, xp, gy + 1), up, down),
            ("x", move(ref, (1, last), (lx + 1, ghost_low), k + 5, xm, gy + 1), up, down),
            ("x", move(ref, (lx, first), (0, ghost_high), k + 6, xp, gy - 1), down, up),
            ("x", move(ref, (1, first), (lx + 1, ghost_high), k + 7, xm, gy - 1), down, up),
        ]

    def field_messages(ref, k):
        def s(a, b):
            return pl.ds(a, b - a)

        return [
            ("x", move(ref, (lx, s(0, 8), mid), (0, s(0, 8), mid), k, xp, gy), None, None),
            ("x", move(ref, (1, s(12, 20), mid), (lx + 1, s(12, 20), mid), k + 1, xm, gy),
             None, None),
            ("x", move(ref, (lx, s(6, 8), last), (0, s(6, 8), ghost_low), k + 2, xp, gy + 1),
             up, down),
            ("x", move(ref, (1, s(12, 14), last), (lx + 1, s(12, 14), ghost_low), k + 3, xm,
                       gy + 1), up, down),
            ("x", move(ref, (lx, s(0, 2), first), (0, s(0, 2), ghost_high), k + 4, xp, gy - 1),
             down, up),
            ("x", move(ref, (1, s(18, 20), first), (lx + 1, s(18, 20), ghost_high), k + 5, xm,
                       gy - 1), down, up),
            ("y", move(ref, (own, s(6, 14), last), (own, s(6, 14), ghost_low), k + 6, gx, gy + 1),
             up, down),
            ("y", move(ref, (own, s(18, 24), first), (own, s(18, 24), ghost_high), k + 7, gx,
                       gy - 1), down, up),
            ("y", move(ref, (own, s(0, 2), first), (own, s(0, 2), ghost_high), k + 8, gx, gy - 1),
             down, up),
        ]

    def each(messages, kind, action):
        for name, copy, sends, receives in messages:
            if kind is not None and name != kind:
                continue
            flag = receives if action == "wait_recv" else sends
            if flag is None:
                getattr(copy, action)()
            else:
                pl.when(flag)(getattr(copy, action))

    pm0, fm0 = phase_messages(p0, 0), field_messages(f0, 8)
    pm1, fm1 = phase_messages(p1, 17), field_messages(f1, 25)

    def loop(kind, body):
        count = {"edge": 2, "inner": lx - 2, "all": lx}[kind]

        def step(t, carry):
            plane, row = t // rt, lax.rem(t, rt)
            if kind == "edge":
                plane = plane * (lx - 1)
            elif kind == "inner":
                plane = plane + 1
            body(plane, pl.multiple_of(row * 8, 8))
            return carry

        lax.fori_loop(0, count * rt, step, 0)

    for x in range(lx):
        p0[1 + x, PAD:top] = jnp.where(labels_ref[x] > 0, 1.0, -1.0).astype(jnp.float32)
    zero = jnp.zeros((8, lz), jnp.float32)

    def rim(flag, slots, rows):
        @pl.when(jnp.logical_not(flag))
        def _():
            for ref in (p0, p1):
                for x in range(lx + 2):
                    ref[x, rows] = zero
            for ref in (f0, f1):
                def fill(x, carry):
                    for s in slots:
                        ref[x, s, rows] = zero
                    return carry
                lax.fori_loop(0, lx + 2, fill, 0)

    rim(down, list(range(6, 14)), slice(0, 8))
    rim(up, list(range(18, 24)) + [0, 1], slice(top, top + 8))

    pl.semaphore_wait(barrier, 2 + 3 * (up.astype(jnp.int32) + down.astype(jnp.int32)))
    each(pm0, None, "start")

    def solid_at(x, r):
        rows = gy * ly + r + lax.broadcasted_iota(jnp.int32, (8, lz), 0)
        return (mask_ref[x, pl.ds(r, 8)] > 0) | (rows == 0) | (rows == ny * ly - 1)

    def collide(ref, x, r, f):
        solid = solid_at(x, r)
        relaxed, rho = relax(f)
        rho_ref[x, pl.ds(r, 8)] = rho
        for i in range(19):
            ref[x + 1, SLOT[i], pl.ds(PAD + r, 8)] = jnp.where(solid, f[OPP[i]], relaxed[i])

    def colour(ref, pref, x, r):
        at = pl.ds(PAD + r, 8)
        up_r, dn_r = pl.ds(PAD + 1 + r, 8), pl.ds(PAD - 1 + r, 8)
        p = pref[x + 1, at]
        e, w = pref[x + 2, at], pref[x, at]
        n, s = pref[x + 1, up_r], pref[x + 1, dn_r]
        ne, se = pref[x + 2, up_r], pref[x + 2, dn_r]
        nw, sw = pref[x, up_r], pref[x, dn_r]

        def zsum(v):
            return pltpu.roll(v, 1, 1) + pltpu.roll(v, lz - 1, 1)

        dx, dy = e - w, n - s
        around = (e + w) + (n + s) + 2.0 * p
        ca, cb = ne - sw, se - nw
        twelfth = 1.0 / 12.0
        hx = (2.0 * dx + zsum(dx) + (ca + cb)) * twelfth
        hy = (2.0 * dy + zsum(dy) + (ca - cb)) * twelfth
        hz = (pltpu.roll(around, lz - 1, 1) - pltpu.roll(around, 1, 1)) * twelfth
        xx, yy, zz = hx * hx, hy * hy, hz * hz
        g2 = (xx + yy) + zz
        inv = lax.rsqrt(jnp.maximum(g2, 0.01))
        inv = jnp.where(solid_at(x, r), 0.0, inv)
        rho = rho_ref[x, pl.ds(r, 8)]
        c18 = (0.1 / 18.0) * inv
        c36 = 0.5 * c18
        k18 = (0.175 / 18.0) * (rho * (1.0 - p * p)) * inv
        k36 = 0.5 * k18
        red = 0.5 + 0.5 * p
        total, reds = {}, {}

        def read(i):
            return ref[x + 1, SLOT[i], at]

        def pair(plus, minus, square, k, along):
            shift = k * along
            for i, sign in ((plus, 1), (minus, -1)):
                value = read(i) + square
                total[i] = value
                reds[i] = red * value + shift if sign > 0 else red * value - shift

        total[0] = read(0) + (6.0 * c18) * g2
        reds[0] = red * total[0]
        pair(1, 2, c18 * (xx - g2), k18, hx)
        pair(3, 4, c18 * (yy - g2), k18, hy)
        pair(5, 6, c18 * (zz - g2), k18, hz)
        for plus, minus, along in ((7, 8, hx + hy), (9, 10, hx - hy), (11, 12, hx + hz),
                                   (13, 14, hx - hz), (15, 16, hy + hz), (17, 18, hy - hz)):
            pair(plus, minus, c36 * (along * along - g2), k36, along)
        sums = {}
        for i, (ex, ey, ez) in enumerate(E):
            value, part = total[i], reds[i]
            if ez != 0:
                value = pltpu.roll(value, ez % lz, 1)
                part = pltpu.roll(part, ez % lz, 1)
            ref[x + 1, SLOT[i], at] = value
            sums[(ex, ey)] = sums[(ex, ey)] + part if (ex, ey) in sums else part
        for key, value in sums.items():
            ref[x + 1, SLOT[key], at] = value

    def pull(ref, x, r, key, ex, ey):
        return ref[x + 1 - ex, SLOT[key], pl.ds(PAD - ey + r, 8)]

    def arrive(ref, x, r):
        return [pull(ref, x, r, i, e[0], e[1]) for i, e in enumerate(E)]

    def tree(values):
        while len(values) > 1:
            values = [sum(values[i:i + 2]) for i in range(0, len(values), 2)]
        return values[0]

    def mix(ref, x, r, f):
        red = tree([pull(ref, x, r, key, *key) for key in RED])
        return 2.0 * red / tree(list(f)) - 1.0

    loop("all", lambda x, r: collide(f0, x, r, [pops_ref[i, x, pl.ds(r, 8)] for i in range(19)]))
    each(pm0, None, "wait_recv")
    loop("edge", functools.partial(colour, f0, p0))
    each(fm0, "x", "start")
    loop("inner", functools.partial(colour, f0, p0))
    each(fm0, "y", "start")
    each(fm0, "y", "wait_recv")

    def inner(x, r):
        f = arrive(f0, x, r)
        p1[x + 1, pl.ds(PAD + r, 8)] = mix(f0, x, r, f)
        collide(f1, x, r, f)

    loop("inner", inner)
    each(fm0, "x", "wait_recv")

    def edge_phase(x, r):
        p1[x + 1, pl.ds(PAD + r, 8)] = mix(f0, x, r, arrive(f0, x, r))

    loop("edge", edge_phase)
    each(pm1, None, "start")
    loop("edge", lambda x, r: collide(f1, x, r, arrive(f0, x, r)))
    each(pm1, None, "wait_recv")
    loop("edge", functools.partial(colour, f1, p1))
    each(fm1, "x", "start")
    loop("inner", functools.partial(colour, f1, p1))
    each(fm1, "y", "start")
    each(fm1, "y", "wait_recv")

    def finish(x, r):
        f = arrive(f1, x, r)
        for i in range(19):
            out_ref[i, x, pl.ds(r, 8)] = f[i]
        phase_ref[x, pl.ds(r, 8)] = mix(f1, x, r, f)

    loop("inner", finish)
    each(fm1, "x", "wait_recv")
    loop("edge", finish)
    for messages in (pm0, fm0, pm1, fm1):
        each(messages, None, "wait_send")


def solution(mesh):
    nx, ny = mesh.shape["gx"], mesh.shape["gy"]

    def on_device(populations, labels, solid_mask):
        lx, ly, lz = labels.shape
        rows = ly + 2 * PAD
        return pl.pallas_call(
            functools.partial(kernel, nx, ny),
            out_shape=(jax.ShapeDtypeStruct((19, lx, ly, lz), jnp.float32),
                       jax.ShapeDtypeStruct((lx, ly, lz), jnp.float32)),
            in_specs=[pl.BlockSpec(memory_space=pltpu.VMEM)] * 3,
            out_specs=(pl.BlockSpec(memory_space=pltpu.VMEM),) * 2,
            scratch_shapes=[
                pltpu.VMEM((lx + 2, NS, rows, lz), jnp.float32),
                pltpu.VMEM((lx + 2, NS, rows, lz), jnp.float32),
                pltpu.VMEM((lx + 2, rows, lz), jnp.float32),
                pltpu.VMEM((lx + 2, rows, lz), jnp.float32),
                pltpu.VMEM((lx, ly, lz), jnp.float32),
                pltpu.SemaphoreType.DMA((34,)),
                pltpu.SemaphoreType.DMA((34,)),
            ],
            compiler_params=pltpu.CompilerParams(
                collective_id=0, has_side_effects=True, vmem_limit_bytes=40 * 2**20),
        )(populations, labels, solid_mask)

    return jax.shard_map(
        on_device, mesh=mesh,
        in_specs=(P(None, "gx", "gy", None), P("gx", "gy", None), P("gx", "gy", None)),
        out_specs=(P(None, "gx", "gy", None), P("gx", "gy", None)),
        check_vma=False)
```

time: 102 us -> 34.9 us (0.34)
  waiting for transfers between devices: 33.6 us -> 0 us
  Pallas kernels: 0 us -> 29.4 us
  starting transfers between devices: 23.5 us -> 0 us
  other arithmetic: 15.6 us -> 0 us
  matrix products: 15.5 us -> 0 us
  local copies, waits for them, and re-layouts: 12.4 us -> 4.63 us
    ppermute x16 -> x0, waiting for transfers between devices: 33.6 us -> none  [the longest x8 19.1 us: with_halo(): lax.ppermute(lax.slice_in_dim(block, block.shape[dim] - width, None, axis...]
    pallas_call x0 -> x1, Pallas kernels: none -> 29.4 us  [on_device(): pl.pallas_call(functools.partial(kernel, nx, ny), out_shape=(jax.ShapeDty...]
    ppermute x16 -> x0, starting transfers between devices: 23.5 us -> none  [the longest x8 16.3 us: with_halo(): lax.ppermute(lax.slice_in_dim(block, 0, width, axis=dim), axis, backward)]
    dot_general x8 -> x0, matrix products: 15.5 us -> none  [the longest x2 6.02 us: collide(): jnp.einsum('ij,j...->i...', collision_k, pops - equilibrium, precision=hi...]
    slice x50 -> x0, local copies, waits for them, and re-layouts: 6.88 us -> none  [the longest x40 3.4 us: on_device(): parts.append(jnp.roll(piece, ez, axis=2))]
    select_n x4 -> x0, other arithmetic: 4.44 us -> none  [the longest x1 2.7 us: collide(): jnp.where(wall_nodes, red_fraction * reflected_populations, separated_col...]
    mul x11 -> x0, other arithmetic: 4.14 us -> none  [the longest x2 2.93 us: on_device(): widened = widened * rim_keep[None, None, :, None]]
    unnamed x39 -> x8, local copies, waits for them, and re-layouts: 0.62 us -> 4.63 us
  transfers between devices with their start and end apart: 16 -> 0, of which waited for: 9 -> 0; matrix products, arithmetic and copies ran while one was open for 17% -> 0% of each run, Pallas kernels for 0% -> 0%
where the time goes in v1:
time: 34.9 us; the launch traced here: 34.6 us
  Pallas kernels  29.4 us (84%)
  local copies, waits for them, and re-layouts  4.63 us (13%)
  between operations  0.65 us (2%)
    pallas_call x1, Pallas kernels, on_device(): pl.pallas_call(functools.partial(kernel, nx, ny), out_shape=(jax.ShapeDty...  29.4 us
    unnamed x8, local copies, waits for them, and re-layouts  4.63 us

profile of v1, /device:TPU:0, one launch (start us, length us, event | category | flops | bytes accessed | tf_op | source)
XLA Modules:
  0.0 34.6 jit_solution(17993397083958226637)
XLA Ops:
  0.6 0.0 copy-start
  0.6 1.3 %copy-done = f32[19,4,32,128]{3,2,1,0:T(8,128)S(1)} copy-done((f32[19,4,32,128]{3,2,1,0:T(8,128)S(1)}, f32[19,4,32,128]{3,2,1,0:T(8,128)}, u32[]{:S(2)}) %copy-start) | copy-done | bytes 1245208
  1.9 0.0 copy-start.1
  1.9 0.8 %copy-done.1 = s32[4,32,128]{2,1,0:T(8,128)S(1)} copy-done((s32[4,32,128]{2,1,0:T(8,128)S(1)}, s32[4,32,128]{2,1,0:T(8,128)}, u32[]{:S(2)}) %copy-start.1) | copy-done | bytes 65560
  2.8 0.0 copy-start.2
  2.8 0.8 %copy-done.2 = s32[4,32,128]{2,1,0:T(8,128)S(1)} copy-done((s32[4,32,128]{2,1,0:T(8,128)S(1)}, s32[4,32,128]{2,1,0:T(8,128)}, u32[]{:S(2)}) %copy-start.2) | copy-done | bytes 65560
  3.6 29.4 %shard_map.50 = (f32[19,4,32,128]{3,2,1,0:T(8,128)S(1)}, f32[4,32,128]{2,1,0:T(8,128)S(1)}) custom-call(f32[19,4,32,128]{3,2,1,0:T(8,128)S(1)} %copy-done, s32[4,32,128]{2,1,0:T(8,128)S(1)} %copy-done.1, s32[4,32,128]{2,1,0:T(8,128)S(1)} %copy-done.2), custom_call_target="tpu_custom_call" | custom-call | tf_op jit(solution)/shard_map/pallas_call | solution.py:341
  33.0 1.0 %copy.7 = f32[19,4,32,128]{3,2,1,0:T(8,128)} copy(f32[19,4,32,128]{3,2,1,0:T(8,128)S(1)} %get-tuple-element.4) | data formatting | bytes 2490368
  34.0 0.6 %copy.8 = f32[4,32,128]{2,1,0:T(8,128)} copy(f32[4,32,128]{2,1,0:T(8,128)S(1)} %get-tuple-element.5) | data formatting | bytes 131072
Async XLA Ops:
  0.6 1.3 %copy-start = (f32[19,4,32,128]{3,2,1,0:T(8,128)S(1)}, f32[19,4,32,128]{3,2,1,0:T(8,128)}, u32[]{:S(2)}) copy-start(f32[19,4,32,128]{3,2,1,0:T(8,128)} %pops_ref.1) | copy-start | bytes 3735556
  1.9 0.8 %copy-start.1 = (s32[4,32,128]{2,1,0:T(8,128)S(1)}, s32[4,32,128]{2,1,0:T(8,128)}, u32[]{:S(2)}) copy-start(s32[4,32,128]{2,1,0:T(8,128)} %labels_ref.1) | copy-start | bytes 196612
  2.8 0.8 %copy-start.2 = (s32[4,32,128]{2,1,0:T(8,128)S(1)}, s32[4,32,128]{2,1,0:T(8,128)}, u32[]{:S(2)}) copy-start(s32[4,32,128]{2,1,0:T(8,128)} %mask_ref.1) | copy-start | bytes 196612

commit v2 on v1

--- a/solution.py
+++ b/solution.py
@@ -49,7 +49,6 @@
     dzz = (sz + (xz[0] + yz[0])) - (third + qz)
     trace = (dxx + dyy) + dzz
     part = trace * (1.0 / 12.0)
-    base = (third + ((qx + qy) + qz)) * (1.0 / 3.0)
     base = rho * (1.0 / 9.0) + ((qx + qy) + qz) * (1.0 / 3.0)
     tx, ty, tz = jx * (1.0 / 3.0), jy * (1.0 / 3.0), jz * (1.0 / 3.0)
     out = list(f)
@@ -84,10 +83,12 @@
     return out, rho
 
 
-def kernel(nx, ny, pops_ref, labels_ref, mask_ref, out_ref, phase_ref,
-           f0, f1, p0, p1, rho_ref, send_sem, recv_sem):
+def kernel(nx, ny, pops_hbm, labels_hbm, mask_hbm, out_ref, phase_ref,
+           f0, f1, p0, p1, rho_ref, pops_ref, labels_ref, mask_ref, load_sem,
+           send_sem, recv_sem):
     lx, ly, lz = labels_ref.shape
-    rt = ly // 8
+    tr = 16 if ly % 16 == 0 else 8
+    rt = ly // tr
     top = PAD + ly
     gx, gy = lax.axis_index("gx"), lax.axis_index("gy")
     xp, xm = lax.rem(gx + 1, nx), lax.rem(gx + nx - 1, nx)
@@ -106,6 +107,17 @@
             greet(gx, ay)
             greet(xp, ay)
             greet(xm, ay)
+
+    def load_plane(x):
+        return pltpu.make_async_copy(pops_hbm.at[:, x], pops_ref.at[:, x], load_sem.at[x])
+
+    load_labels = pltpu.make_async_copy(labels_hbm, labels_ref, load_sem.at[lx])
+    load_mask = pltpu.make_async_copy(mask_hbm, mask_ref, load_sem.at[lx + 1])
+    load_labels.start()
+    for x in range(lx):
+        load_plane(x).start()
+        if x == 0:
+            load_mask.start()
 
     def move(ref, src, dst, k, ax, ay):
         return pltpu.make_async_remote_copy(
@@ -176,13 +188,11 @@
                 plane = plane * (lx - 1)
             elif kind == "inner":
                 plane = plane + 1
-            body(plane, pl.multiple_of(row * 8, 8))
+            body(plane, pl.multiple_of(row * tr, 8))
             return carry
 
         lax.fori_loop(0, count * rt, step, 0)
 
-    for x in range(lx):
-        p0[1 + x, PAD:top] = jnp.where(labels_ref[x] > 0, 1.0, -1.0).astype(jnp.float32)
     zero = jnp.zeros((8, lz), jnp.float32)
 
     def rim(flag, slots, rows):
@@ -201,23 +211,26 @@
     rim(down, list(range(6, 14)), slice(0, 8))
     rim(up, list(range(18, 24)) + [0, 1], slice(top, top + 8))
 
+    load_labels.wait()
+    for x in range(lx):
+        p0[1 + x, PAD:top] = jnp.where(labels_ref[x] > 0, 1.0, -1.0).astype(jnp.float32)
     pl.semaphore_wait(barrier, 2 + 3 * (up.astype(jnp.int32) + down.astype(jnp.int32)))
     each(pm0, None, "start")
 
     def solid_at(x, r):
-        rows = gy * ly + r + lax.broadcasted_iota(jnp.int32, (8, lz), 0)
-        return (mask_ref[x, pl.ds(r, 8)] > 0) | (rows == 0) | (rows == ny * ly - 1)
+        rows = gy * ly + r + lax.broadcasted_iota(jnp.int32, (tr, lz), 0)
+        return (mask_ref[x, pl.ds(r, tr)] > 0) | (rows == 0) | (rows == ny * ly - 1)
 
     def collide(ref, x, r, f):
         solid = solid_at(x, r)
         relaxed, rho = relax(f)
-        rho_ref[x, pl.ds(r, 8)] = rho
+        rho_ref[x, pl.ds(r, tr)] = rho
         for i in range(19):
-            ref[x + 1, SLOT[i], pl.ds(PAD + r, 8)] = jnp.where(solid, f[OPP[i]], relaxed[i])
+            ref[x + 1, SLOT[i], pl.ds(PAD + r, tr)] = jnp.where(solid, f[OPP[i]], relaxed[i])
 
     def colour(ref, pref, x, r):
-        at = pl.ds(PAD + r, 8)
-        up_r, dn_r = pl.ds(PAD + 1 + r, 8), pl.ds(PAD - 1 + r, 8)
+        at = pl.ds(PAD + r, tr)
+        up_r, dn_r = pl.ds(PAD + 1 + r, tr), pl.ds(PAD - 1 + r, tr)
         p = pref[x + 1, at]
         e, w = pref[x + 2, at], pref[x, at]
         n, s = pref[x + 1, up_r], pref[x + 1, dn_r]
@@ -238,7 +251,7 @@
         g2 = (xx + yy) + zz
         inv = lax.rsqrt(jnp.maximum(g2, 0.01))
         inv = jnp.where(solid_at(x, r), 0.0, inv)
-        rho = rho_ref[x, pl.ds(r, 8)]
+        rho = rho_ref[x, pl.ds(r, tr)]
         c18 = (0.1 / 18.0) * inv
         c36 = 0.5 * c18
         k18 = (0.175 / 18.0) * (rho * (1.0 - p * p)) * inv
@@ -276,7 +289,7 @@
             ref[x + 1, SLOT[key], at] = value
 
     def pull(ref, x, r, key, ex, ey):
-        return ref[x + 1 - ex, SLOT[key], pl.ds(PAD - ey + r, 8)]
+        return ref[x + 1 - ex, SLOT[key], pl.ds(PAD - ey + r, tr)]
 
     def arrive(ref, x, r):
         return [pull(ref, x, r, i, e[0], e[1]) for i, e in enumerate(E)]
@@ -290,7 +303,19 @@
         red = tree([pull(ref, x, r, key, *key) for key in RED])
         return 2.0 * red / tree(list(f)) - 1.0
 
-    loop("all", lambda x, r: collide(f0, x, r, [pops_ref[i, x, pl.ds(r, 8)] for i in range(19)]))
+    load_mask.wait()
+
+    def first_plane(x, carry):
+        load_plane(x).wait()
+
+        def step(t, carry):
+            r = pl.multiple_of(t * tr, 8)
+            collide(f0, x, r, [pops_ref[i, x, pl.ds(r, tr)] for i in range(19)])
+            return carry
+
+        return lax.fori_loop(0, rt, step, carry)
+
+    lax.fori_loop(0, lx, first_plane, 0)
     each(pm0, None, "wait_recv")
     loop("edge", functools.partial(colour, f0, p0))
     each(fm0, "x", "start")
@@ -300,14 +325,14 @@
 
     def inner(x, r):
         f = arrive(f0, x, r)
-        p1[x + 1, pl.ds(PAD + r, 8)] = mix(f0, x, r, f)
+        p1[x + 1, pl.ds(PAD + r, tr)] = mix(f0, x, r, f)
         collide(f1, x, r, f)
 
     loop("inner", inner)
     each(fm0, "x", "wait_recv")
 
     def edge_phase(x, r):
-        p1[x + 1, pl.ds(PAD + r, 8)] = mix(f0, x, r, arrive(f0, x, r))
+        p1[x + 1, pl.ds(PAD + r, tr)] = mix(f0, x, r, arrive(f0, x, r))
 
     loop("edge", edge_phase)
     each(pm1, None, "start")
@@ -322,8 +347,8 @@
     def finish(x, r):
         f = arrive(f1, x, r)
         for i in range(19):
-            out_ref[i, x, pl.ds(r, 8)] = f[i]
-        phase_ref[x, pl.ds(r, 8)] = mix(f1, x, r, f)
+            out_ref[i, x, pl.ds(r, tr)] = f[i]
+        phase_ref[x, pl.ds(r, tr)] = mix(f1, x, r, f)
 
     loop("inner", finish)
     each(fm1, "x", "wait_recv")
@@ -342,7 +367,7 @@
             functools.partial(kernel, nx, ny),
             out_shape=(jax.ShapeDtypeStruct((19, lx, ly, lz), jnp.float32),
                        jax.ShapeDtypeStruct((lx, ly, lz), jnp.float32)),
-            in_specs=[pl.BlockSpec(memory_space=pltpu.VMEM)] * 3,
+            in_specs=[pl.BlockSpec(memory_space=pltpu.HBM)] * 3,
             out_specs=(pl.BlockSpec(memory_space=pltpu.VMEM),) * 2,
             scratch_shapes=[
                 pltpu.VMEM((lx + 2, NS, rows, lz), jnp.float32),
@@ -350,6 +375,10 @@
                 pltpu.VMEM((lx + 2, rows, lz), jnp.float32),
                 pltpu.VMEM((lx + 2, rows, lz), jnp.float32),
                 pltpu.VMEM((lx, ly, lz), jnp.float32),
+                pltpu.VMEM((19, lx, ly, lz), jnp.float32),
+                pltpu.VMEM((lx, ly, lz), jnp.int32),
+                pltpu.VMEM((lx, ly, lz), jnp.int32),
+                pltpu.SemaphoreType.DMA((lx + 2,)),
                 pltpu.SemaphoreType.DMA((34,)),
                 pltpu.SemaphoreType.DMA((34,)),
             ],

time: 34.9 us -> 33.7 us (0.966)
  Pallas kernels: 29.4 us -> 28.2 us
    pallas_call x1, Pallas kernels: 29.4 us -> 28.2 us  [on_device(): pl.pallas_call(functools.partial(kernel, nx, ny), out_shape=(jax.ShapeDty...]
where the time goes in v2:
time: 33.7 us; the launch traced here: 33.4 us
  Pallas kernels  28.2 us (84%)
  local copies, waits for them, and re-layouts  4.63 us (14%)
  between operations  0.65 us (2%)
    pallas_call x1, Pallas kernels, on_device(): pl.pallas_call(functools.partial(kernel, nx, ny), out_shape=(jax.ShapeDty...  28.2 us
    unnamed x8, local copies, waits for them, and re-layouts  4.63 us

profile of v2, /device:TPU:0, one launch (start us, length us, event | category | flops | bytes accessed | tf_op | source)
XLA Modules:
  0.0 33.4 jit_solution(10722759583329185981)
XLA Ops:
  0.6 0.0 copy-start
  0.6 1.3 %copy-done = f32[19,4,32,128]{3,2,1,0:T(8,128)S(1)} copy-done((f32[19,4,32,128]{3,2,1,0:T(8,128)S(1)}, f32[19,4,32,128]{3,2,1,0:T(8,128)}, u32[]{:S(2)}) %copy-start) | copy-done | bytes 1245208
  1.9 0.0 copy-start.1
  1.9 0.8 %copy-done.1 = s32[4,32,128]{2,1,0:T(8,128)S(1)} copy-done((s32[4,32,128]{2,1,0:T(8,128)S(1)}, s32[4,32,128]{2,1,0:T(8,128)}, u32[]{:S(2)}) %copy-start.1) | copy-done | bytes 65560
  2.8 0.0 copy-start.2
  2.8 0.8 %copy-done.2 = s32[4,32,128]{2,1,0:T(8,128)S(1)} copy-done((s32[4,32,128]{2,1,0:T(8,128)S(1)}, s32[4,32,128]{2,1,0:T(8,128)}, u32[]{:S(2)}) %copy-start.2) | copy-done | bytes 65560
  3.6 28.2 %shard_map.50 = (f32[19,4,32,128]{3,2,1,0:T(8,128)S(1)}, f32[4,32,128]{2,1,0:T(8,128)S(1)}) custom-call(f32[19,4,32,128]{3,2,1,0:T(8,128)S(1)} %copy-done, s32[4,32,128]{2,1,0:T(8,128)S(1)} %copy-done.1, s32[4,32,128]{2,1,0:T(8,128)S(1)} %copy-done.2), custom_call_target="tpu_custom_call" | custom-call | tf_op jit(solution)/shard_map/pallas_call | solution.py:366
  31.8 1.0 %copy.7 = f32[19,4,32,128]{3,2,1,0:T(8,128)} copy(f32[19,4,32,128]{3,2,1,0:T(8,128)S(1)} %get-tuple-element.4) | data formatting | bytes 2490368
  32.8 0.6 %copy.8 = f32[4,32,128]{2,1,0:T(8,128)} copy(f32[4,32,128]{2,1,0:T(8,128)S(1)} %get-tuple-element.5) | data formatting | bytes 131072
Async XLA Ops:
  0.6 1.3 %copy-start = (f32[19,4,32,128]{3,2,1,0:T(8,128)S(1)}, f32[19,4,32,128]{3,2,1,0:T(8,128)}, u32[]{:S(2)}) copy-start(f32[19,4,32,128]{3,2,1,0:T(8,128)} %pops_hbm.1) | copy-start | bytes 3735556
  1.9 0.8 %copy-start.1 = (s32[4,32,128]{2,1,0:T(8,128)S(1)}, s32[4,32,128]{2,1,0:T(8,128)}, u32[]{:S(2)}) copy-start(s32[4,32,128]{2,1,0:T(8,128)} %labels_hbm.1) | copy-start | bytes 196612
  2.8 0.8 %copy-start.2 = (s32[4,32,128]{2,1,0:T(8,128)S(1)}, s32[4,32,128]{2,1,0:T(8,128)}, u32[]{:S(2)}) copy-start(s32[4,32,128]{2,1,0:T(8,128)} %mask_hbm.1) | copy-start | bytes 196612

commit v3 on v2

--- a/solution.py
+++ b/solution.py
@@ -14,8 +14,8 @@
 ]
 OPP = [0, 2, 1, 4, 3, 6, 5, 8, 7, 10, 9, 12, 11, 14, 13, 16, 15, 18, 17]
 ORDER = [
-    9, (1, -1), 1, 11, 13, (1, 0), 7, (1, 1),
-    3, 15, 17, (0, 1), 10, (-1, 1),
+    (1, -1), 9, 1, 11, 13, (1, 0), 7, (1, 1),
+    3, 15, 17, (0, 1), (-1, 1), 10,
     2, 12, 14, (-1, 0), 8, (-1, -1),
     4, 16, 18, (0, -1),
     0, 5, 6, (0, 0),
@@ -83,9 +83,9 @@
     return out, rho
 
 
-def kernel(nx, ny, pops_hbm, labels_hbm, mask_hbm, out_ref, phase_ref,
-           f0, f1, p0, p1, rho_ref, pops_ref, labels_ref, mask_ref, load_sem,
-           send_sem, recv_sem):
+def kernel(nx, ny, pops_hbm, labels_hbm, mask_hbm, out_hbm, phase_hbm,
+           f0, f1, p0, p1, rho_ref, pops_ref, labels_ref, mask_ref, y0, y1, load_sem,
+           store_sem, send_sem, recv_sem):
     lx, ly, lz = labels_ref.shape
     tr = 16 if ly % 16 == 0 else 8
     rt = ly // tr
@@ -142,13 +142,13 @@
             ("x", move(ref, (1, first), (lx + 1, ghost_high), k + 7, xm, gy - 1), down, up),
         ]
 
-    def field_messages(ref, k):
+    def field_messages(ref, rows, k):
         def s(a, b):
             return pl.ds(a, b - a)
 
         return [
-            ("x", move(ref, (lx, s(0, 8), mid), (0, s(0, 8), mid), k, xp, gy), None, None),
-            ("x", move(ref, (1, s(12, 20), mid), (lx + 1, s(12, 20), mid), k + 1, xm, gy),
+            ("x", move(ref, (lx, s(1, 7), mid), (0, s(1, 7), mid), k, xp, gy), None, None),
+            ("x", move(ref, (1, s(13, 19), mid), (lx + 1, s(13, 19), mid), k + 1, xm, gy),
              None, None),
             ("x", move(ref, (lx, s(6, 8), last), (0, s(6, 8), ghost_low), k + 2, xp, gy + 1),
              up, down),
@@ -158,13 +158,34 @@
              down, up),
             ("x", move(ref, (1, s(18, 20), first), (lx + 1, s(18, 20), ghost_high), k + 5, xm,
                        gy - 1), down, up),
-            ("y", move(ref, (own, s(6, 14), last), (own, s(6, 14), ghost_low), k + 6, gx, gy + 1),
-             up, down),
-            ("y", move(ref, (own, s(18, 24), first), (own, s(18, 24), ghost_high), k + 7, gx,
-                       gy - 1), down, up),
-            ("y", move(ref, (own, s(0, 2), first), (own, s(0, 2), ghost_high), k + 8, gx, gy - 1),
-             down, up),
+            ("y", move(rows, 0, 1, k + 6, gx, gy + 1), up, down),
+            ("y", move(rows, 2, 3, k + 7, gx, gy - 1), down, up),
         ]
+
+    upward = list(range(6, 14))
+    downward = list(range(18, 24)) + [0, 1]
+
+    def pack(ref, rows):
+        for flag, slots, place, row in ((up, upward, 0, top - 1), (down, downward, 2, PAD)):
+            @pl.when(flag)
+            def _():
+                for x in range(lx):
+                    for k, slot in enumerate(slots):
+                        rows[place, x, k:k + 1] = ref[x + 1, slot, row:row + 1]
+
+    def unpack(ref, rows):
+        for flag, slots, place, row in ((down, upward, 1, PAD - 1), (up, downward, 3, top)):
+            @pl.when(flag)
+            def _():
+                for x in range(lx):
+                    for k, slot in enumerate(slots):
+                        ref[x + 1, slot, row:row + 1] = rows[place, x, k:k + 1]
+
+    def gather_red(ref):
+        for x, ex in ((lx, 1), (1, -1)):
+            ref[x, SLOT[(ex, 0)], PAD:top] = (
+                ref[x, SLOT[(ex, 0)], PAD:top] + ref[x, SLOT[(ex, 1)], PAD - 1:top - 1]
+                + ref[x, SLOT[(ex, -1)], PAD + 1:top + 1])
 
     def each(messages, kind, action):
         for name, copy, sends, receives in messages:
@@ -176,8 +197,8 @@
             else:
                 pl.when(flag)(getattr(copy, action))
 
-    pm0, fm0 = phase_messages(p0, 0), field_messages(f0, 8)
-    pm1, fm1 = phase_messages(p1, 17), field_messages(f1, 25)
+    pm0, fm0 = phase_messages(p0, 0), field_messages(f0, y0, 8)
+    pm1, fm1 = phase_messages(p1, 16), field_messages(f1, y1, 24)
 
     def loop(kind, body):
         count = {"edge": 2, "inner": lx - 2, "all": lx}[kind]
@@ -195,21 +216,25 @@
 
     zero = jnp.zeros((8, lz), jnp.float32)
 
-    def rim(flag, slots, rows):
+    def fill(x, carry):
+        for ref in (f0, f1):
+            for slot in upward:
+                ref[x, slot, 0:8] = zero
+            for slot in downward:
+                ref[x, slot, top:top + 8] = zero
+        return carry
+
+    lax.fori_loop(0, lx + 2, fill, 0)
+    for ref in (f0, f1):
+        for x, ex in ((0, 1), (lx + 1, -1)):
+            for ey in (1, -1):
+                ref[x, SLOT[(ex, ey)], PAD:top] = jnp.zeros((ly, lz), jnp.float32)
+    for flag, rows in ((down, slice(0, 8)), (up, slice(top, top + 8))):
         @pl.when(jnp.logical_not(flag))
         def _():
             for ref in (p0, p1):
                 for x in range(lx + 2):
                     ref[x, rows] = zero
-            for ref in (f0, f1):
-                def fill(x, carry):
-                    for s in slots:
-                        ref[x, s, rows] = zero
-                    return carry
-                lax.fori_loop(0, lx + 2, fill, 0)
-
-    rim(down, list(range(6, 14)), slice(0, 8))
-    rim(up, list(range(18, 24)) + [0, 1], slice(top, top + 8))
 
     load_labels.wait()
     for x in range(lx):
@@ -318,10 +343,13 @@
     lax.fori_loop(0, lx, first_plane, 0)
     each(pm0, None, "wait_recv")
     loop("edge", functools.partial(colour, f0, p0))
+    gather_red(f0)
     each(fm0, "x", "start")
     loop("inner", functools.partial(colour, f0, p0))
+    pack(f0, y0)
     each(fm0, "y", "start")
     each(fm0, "y", "wait_recv")
+    unpack(f0, y0)
 
     def inner(x, r):
         f = arrive(f0, x, r)
@@ -339,22 +367,45 @@
     loop("edge", lambda x, r: collide(f1, x, r, arrive(f0, x, r)))
     each(pm1, None, "wait_recv")
     loop("edge", functools.partial(colour, f1, p1))
+    gather_red(f1)
     each(fm1, "x", "start")
     loop("inner", functools.partial(colour, f1, p1))
+    pack(f1, y1)
     each(fm1, "y", "start")
     each(fm1, "y", "wait_recv")
-
-    def finish(x, r):
-        f = arrive(f1, x, r)
-        for i in range(19):
-            out_ref[i, x, pl.ds(r, tr)] = f[i]
-        phase_ref[x, pl.ds(r, tr)] = mix(f1, x, r, f)
-
-    loop("inner", finish)
+    unpack(f1, y1)
+
+    def store_plane(x):
+        return pltpu.make_async_copy(pops_ref.at[:, x], out_hbm.at[:, x], store_sem.at[x])
+
+    def finish(first_x, stride, count):
+        def plane(n, carry):
+            x = first_x + n * stride
+
+            def step(t, carry):
+                r = pl.multiple_of(t * tr, 8)
+                f = arrive(f1, x, r)
+                for i in range(19):
+                    pops_ref[i, x, pl.ds(r, tr)] = f[i]
+                rho_ref[x, pl.ds(r, tr)] = mix(f1, x, r, f)
+                return carry
+
+            lax.fori_loop(0, rt, step, 0)
+            store_plane(x).start()
+            return carry
+
+        lax.fori_loop(0, count, plane, 0)
+
+    finish(1, 1, lx - 2)
     each(fm1, "x", "wait_recv")
-    loop("edge", finish)
+    finish(0, lx - 1, 2)
+    store_phase = pltpu.make_async_copy(rho_ref, phase_hbm, store_sem.at[lx])
+    store_phase.start()
     for messages in (pm0, fm0, pm1, fm1):
         each(messages, None, "wait_send")
+    for x in range(lx):
+        store_plane(x).wait()
+    store_phase.wait()
 
 
 def solution(mesh):
@@ -368,7 +419,7 @@
             out_shape=(jax.ShapeDtypeStruct((19, lx, ly, lz), jnp.float32),
                        jax.ShapeDtypeStruct((lx, ly, lz), jnp.float32)),
             in_specs=[pl.BlockSpec(memory_space=pltpu.HBM)] * 3,
-            out_specs=(pl.BlockSpec(memory_space=pltpu.VMEM),) * 2,
+            out_specs=(pl.BlockSpec(memory_space=pltpu.HBM),) * 2,
             scratch_shapes=[
                 pltpu.VMEM((lx + 2, NS, rows, lz), jnp.float32),
                 pltpu.VMEM((lx + 2, NS, rows, lz), jnp.float32),
@@ -378,12 +429,15 @@
                 pltpu.VMEM((19, lx, ly, lz), jnp.float32),
                 pltpu.VMEM((lx, ly, lz), jnp.int32),
                 pltpu.VMEM((lx, ly, lz), jnp.int32),
+                pltpu.VMEM((4, lx, 8, lz), jnp.float32),
+                pltpu.VMEM((4, lx, 8, lz), jnp.float32),
                 pltpu.SemaphoreType.DMA((lx + 2,)),
-                pltpu.SemaphoreType.DMA((34,)),
-                pltpu.SemaphoreType.DMA((34,)),
+                pltpu.SemaphoreType.DMA((lx + 1,)),
+                pltpu.SemaphoreType.DMA((32,)),
+                pltpu.SemaphoreType.DMA((32,)),
             ],
             compiler_params=pltpu.CompilerParams(
-                collective_id=0, has_side_effects=True, vmem_limit_bytes=40 * 2**20),
+                collective_id=0, has_side_effects=True, vmem_limit_bytes=64 * 2**20),
         )(populations, labels, solid_mask)
 
     return jax.shard_map(

time: 33.7 us -> 32.1 us (0.953)
  local copies, waits for them, and re-layouts: 4.63 us -> 3.12 us
    unnamed x8 -> x4, local copies, waits for them, and re-layouts: 4.63 us -> 3.12 us
where the time goes in v3:
time: 32.1 us; the launch traced here: 32 us
  Pallas kernels  28.2 us (88%)
  local copies, waits for them, and re-layouts  3.12 us (10%)
  between operations  0.65 us (2%)
    pallas_call x1, Pallas kernels, on_device(): pl.pallas_call(functools.partial(kernel, nx, ny), out_shape=(jax.ShapeDty...  28.2 us
    unnamed x4, local copies, waits for them, and re-layouts  3.12 us

profile of v3, /device:TPU:0, one launch (start us, length us, event | category | flops | bytes accessed | tf_op | source)
XLA Modules:
  0.0 32.0 jit_solution(5350478326159928582)
XLA Ops:
  0.6 28.2 %shard_map.50 = (f32[19,4,32,128]{3,2,1,0:T(8,128)}, f32[4,32,128]{2,1,0:T(8,128)}) custom-call(f32[19,4,32,128]{3,2,1,0:T(8,128)} %pops_hbm.1, s32[4,32,128]{2,1,0:T(8,128)} %labels_hbm.1, s32[4,32,128]{2,1,0:T(8,128)} %mask_hbm.1), custom_call_target="tpu_custom_call" | custom-call | tf_op jit(solution)/shard_map/pallas_call | solution.py:417
  28.8 0.0 copy-start
  28.8 2.5 %copy.7 = f32[19,4,32,128]{3,2,1,0:T(8,128)} copy(f32[19,4,32,128]{3,2,1,0:T(8,128)} %get-tuple-element.4) | data formatting | bytes 2490368
  31.3 0.0 copy-done
  31.3 0.6 %copy.8 = f32[4,32,128]{2,1,0:T(8,128)} copy(f32[4,32,128]{2,1,0:T(8,128)S(1)} %copy-done) | data formatting | bytes 131072
Async XLA Ops:
  28.8 2.5 %copy-start = (f32[4,32,128]{2,1,0:T(8,128)S(1)}, f32[4,32,128]{2,1,0:T(8,128)}, u32[]{:S(2)}) copy-start(f32[4,32,128]{2,1,0:T(8,128)} %get-tuple-element.5) | copy-start | bytes 196612

commit v4 on v3

--- a/solution.py
+++ b/solution.py
@@ -83,11 +83,11 @@
     return out, rho
 
 
-def kernel(nx, ny, pops_hbm, labels_hbm, mask_hbm, out_hbm, phase_hbm,
-           f0, f1, p0, p1, rho_ref, pops_ref, labels_ref, mask_ref, y0, y1, load_sem,
-           store_sem, send_sem, recv_sem):
-    lx, ly, lz = labels_ref.shape
-    tr = 16 if ly % 16 == 0 else 8
+def kernel(nx, ny, pops_hbm, code_ref, out_ref, phase_ref,
+           f0, f1, p0, p1, rho_ref, pops_ref, y0, y1, load_sem,
+           send_sem, recv_sem):
+    lx, ly, lz = code_ref.shape
+    tr = 32 if ly % 32 == 0 else 8
     rt = ly // tr
     top = PAD + ly
     gx, gy = lax.axis_index("gx"), lax.axis_index("gy")
@@ -111,13 +111,8 @@
     def load_plane(x):
         return pltpu.make_async_copy(pops_hbm.at[:, x], pops_ref.at[:, x], load_sem.at[x])
 
-    load_labels = pltpu.make_async_copy(labels_hbm, labels_ref, load_sem.at[lx])
-    load_mask = pltpu.make_async_copy(mask_hbm, mask_ref, load_sem.at[lx + 1])
-    load_labels.start()
     for x in range(lx):
         load_plane(x).start()
-        if x == 0:
-            load_mask.start()
 
     def move(ref, src, dst, k, ax, ay):
         return pltpu.make_async_remote_copy(
@@ -147,16 +142,16 @@
             return pl.ds(a, b - a)
 
         return [
-            ("x", move(ref, (lx, s(1, 7), mid), (0, s(1, 7), mid), k, xp, gy), None, None),
-            ("x", move(ref, (1, s(13, 19), mid), (lx + 1, s(13, 19), mid), k + 1, xm, gy),
+            ("x+", move(ref, (lx, s(1, 7), mid), (0, s(1, 7), mid), k, xp, gy), None, None),
+            ("x-", move(ref, (1, s(13, 19), mid), (lx + 1, s(13, 19), mid), k + 1, xm, gy),
              None, None),
-            ("x", move(ref, (lx, s(6, 8), last), (0, s(6, 8), ghost_low), k + 2, xp, gy + 1),
+            ("x+", move(ref, (lx, s(6, 8), last), (0, s(6, 8), ghost_low), k + 2, xp, gy + 1),
              up, down),
-            ("x", move(ref, (1, s(12, 14), last), (lx + 1, s(12, 14), ghost_low), k + 3, xm,
+            ("x-", move(ref, (1, s(12, 14), last), (lx + 1, s(12, 14), ghost_low), k + 3, xm,
                        gy + 1), up, down),
-            ("x", move(ref, (lx, s(0, 2), first), (0, s(0, 2), ghost_high), k + 4, xp, gy - 1),
+            ("x+", move(ref, (lx, s(0, 2), first), (0, s(0, 2), ghost_high), k + 4, xp, gy - 1),
              down, up),
-            ("x", move(ref, (1, s(18, 20), first), (lx + 1, s(18, 20), ghost_high), k + 5, xm,
+            ("x-", move(ref, (1, s(18, 20), first), (lx + 1, s(18, 20), ghost_high), k + 5, xm,
                        gy - 1), down, up),
             ("y", move(rows, 0, 1, k + 6, gx, gy + 1), up, down),
             ("y", move(rows, 2, 3, k + 7, gx, gy - 1), down, up),
@@ -181,15 +176,14 @@
                     for k, slot in enumerate(slots):
                         ref[x + 1, slot, row:row + 1] = rows[place, x, k:k + 1]
 
-    def gather_red(ref):
-        for x, ex in ((lx, 1), (1, -1)):
-            ref[x, SLOT[(ex, 0)], PAD:top] = (
-                ref[x, SLOT[(ex, 0)], PAD:top] + ref[x, SLOT[(ex, 1)], PAD - 1:top - 1]
-                + ref[x, SLOT[(ex, -1)], PAD + 1:top + 1])
+    def gather_red(ref, x, ex):
+        ref[x, SLOT[(ex, 0)], PAD:top] = (
+            ref[x, SLOT[(ex, 0)], PAD:top] + ref[x, SLOT[(ex, 1)], PAD - 1:top - 1]
+            + ref[x, SLOT[(ex, -1)], PAD + 1:top + 1])
 
     def each(messages, kind, action):
         for name, copy, sends, receives in messages:
-            if kind is not None and name != kind:
+            if kind is not None and kind not in name:
                 continue
             flag = receives if action == "wait_recv" else sends
             if flag is None:
@@ -201,12 +195,14 @@
     pm1, fm1 = phase_messages(p1, 16), field_messages(f1, y1, 24)
 
     def loop(kind, body):
-        count = {"edge": 2, "inner": lx - 2, "all": lx}[kind]
+        count = {"edge": 2, "inner": lx - 2, "low": 1, "high": 1}[kind]
 
         def step(t, carry):
             plane, row = t // rt, lax.rem(t, rt)
             if kind == "edge":
                 plane = plane * (lx - 1)
+            elif kind == "high":
+                plane = plane + (lx - 1)
             elif kind == "inner":
                 plane = plane + 1
             body(plane, pl.multiple_of(row * tr, 8))
@@ -236,15 +232,13 @@
                 for x in range(lx + 2):
                     ref[x, rows] = zero
 
-    load_labels.wait()
     for x in range(lx):
-        p0[1 + x, PAD:top] = jnp.where(labels_ref[x] > 0, 1.0, -1.0).astype(jnp.float32)
+        p0[1 + x, PAD:top] = jnp.where((code_ref[x] & 1) > 0, 1.0, -1.0).astype(jnp.float32)
     pl.semaphore_wait(barrier, 2 + 3 * (up.astype(jnp.int32) + down.astype(jnp.int32)))
     each(pm0, None, "start")
 
     def solid_at(x, r):
-        rows = gy * ly + r + lax.broadcasted_iota(jnp.int32, (tr, lz), 0)
-        return (mask_ref[x, pl.ds(r, tr)] > 0) | (rows == 0) | (rows == ny * ly - 1)
+        return code_ref[x, pl.ds(r, tr)] > 1
 
     def collide(ref, x, r, f):
         solid = solid_at(x, r)
@@ -328,7 +322,6 @@
         red = tree([pull(ref, x, r, key, *key) for key in RED])
         return 2.0 * red / tree(list(f)) - 1.0
 
-    load_mask.wait()
 
     def first_plane(x, carry):
         load_plane(x).wait()
@@ -342,9 +335,10 @@
 
     lax.fori_loop(0, lx, first_plane, 0)
     each(pm0, None, "wait_recv")
-    loop("edge", functools.partial(colour, f0, p0))
-    gather_red(f0)
-    each(fm0, "x", "start")
+    for side, x, ex, name in (("high", lx, 1, "x+"), ("low", 1, -1, "x-")):
+        loop(side, functools.partial(colour, f0, p0))
+        gather_red(f0, x, ex)
+        each(fm0, name, "start")
     loop("inner", functools.partial(colour, f0, p0))
     pack(f0, y0)
     each(fm0, "y", "start")
@@ -366,18 +360,16 @@
     each(pm1, None, "start")
     loop("edge", lambda x, r: collide(f1, x, r, arrive(f0, x, r)))
     each(pm1, None, "wait_recv")
-    loop("edge", functools.partial(colour, f1, p1))
-    gather_red(f1)
-    each(fm1, "x", "start")
+    for side, x, ex, name in (("high", lx, 1, "x+"), ("low", 1, -1, "x-")):
+        loop(side, functools.partial(colour, f1, p1))
+        gather_red(f1, x, ex)
+        each(fm1, name, "start")
     loop("inner", functools.partial(colour, f1, p1))
     pack(f1, y1)
     each(fm1, "y", "start")
     each(fm1, "y", "wait_recv")
     unpack(f1, y1)
 
-    def store_plane(x):
-        return pltpu.make_async_copy(pops_ref.at[:, x], out_hbm.at[:, x], store_sem.at[x])
-
     def finish(first_x, stride, count):
         def plane(n, carry):
             x = first_x + n * stride
@@ -386,26 +378,19 @@
                 r = pl.multiple_of(t * tr, 8)
                 f = arrive(f1, x, r)
                 for i in range(19):
-                    pops_ref[i, x, pl.ds(r, tr)] = f[i]
-                rho_ref[x, pl.ds(r, tr)] = mix(f1, x, r, f)
+                    out_ref[i, x, pl.ds(r, tr)] = f[i]
+                phase_ref[x, pl.ds(r, tr)] = mix(f1, x, r, f)
                 return carry
 
-            lax.fori_loop(0, rt, step, 0)
-            store_plane(x).start()
-            return carry
+            return lax.fori_loop(0, rt, step, carry)
 
         lax.fori_loop(0, count, plane, 0)
 
     finish(1, 1, lx - 2)
     each(fm1, "x", "wait_recv")
     finish(0, lx - 1, 2)
-    store_phase = pltpu.make_async_copy(rho_ref, phase_hbm, store_sem.at[lx])
-    store_phase.start()
     for messages in (pm0, fm0, pm1, fm1):
         each(messages, None, "wait_send")
-    for x in range(lx):
-        store_plane(x).wait()
-    store_phase.wait()
 
 
 def solution(mesh):
@@ -414,12 +399,15 @@
     def on_device(populations, labels, solid_mask):
         lx, ly, lz = labels.shape
         rows = ly + 2 * PAD
+        y = lax.axis_index("gy") * ly + lax.broadcasted_iota(jnp.int32, (lx, ly, lz), 1)
+        solid = (solid_mask > 0) | (y == 0) | (y == ny * ly - 1)
+        code = jnp.where(labels > 0, 1, 0) + jnp.where(solid, 2, 0)
         return pl.pallas_call(
             functools.partial(kernel, nx, ny),
             out_shape=(jax.ShapeDtypeStruct((19, lx, ly, lz), jnp.float32),
                        jax.ShapeDtypeStruct((lx, ly, lz), jnp.float32)),
-            in_specs=[pl.BlockSpec(memory_space=pltpu.HBM)] * 3,
-            out_specs=(pl.BlockSpec(memory_space=pltpu.HBM),) * 2,
+            in_specs=[pl.BlockSpec(memory_space=pltpu.HBM), pl.BlockSpec(memory_space=pltpu.VMEM)],
+            out_specs=(pl.BlockSpec(memory_space=pltpu.VMEM),) * 2,
             scratch_shapes=[
                 pltpu.VMEM((lx + 2, NS, rows, lz), jnp.float32),
                 pltpu.VMEM((lx + 2, NS, rows, lz), jnp.float32),
@@ -427,18 +415,15 @@
                 pltpu.VMEM((lx + 2, rows, lz), jnp.float32),
                 pltpu.VMEM((lx, ly, lz), jnp.float32),
                 pltpu.VMEM((19, lx, ly, lz), jnp.float32),
-                pltpu.VMEM((lx, ly, lz), jnp.int32),
-                pltpu.VMEM((lx, ly, lz), jnp.int32),
                 pltpu.VMEM((4, lx, 8, lz), jnp.float32),
                 pltpu.VMEM((4, lx, 8, lz), jnp.float32),
-                pltpu.SemaphoreType.DMA((lx + 2,)),
-                pltpu.SemaphoreType.DMA((lx + 1,)),
+                pltpu.SemaphoreType.DMA((lx,)),
                 pltpu.SemaphoreType.DMA((32,)),
                 pltpu.SemaphoreType.DMA((32,)),
             ],
             compiler_params=pltpu.CompilerParams(
-                collective_id=0, has_side_effects=True, vmem_limit_bytes=64 * 2**20),
-        )(populations, labels, solid_mask)
+                collective_id=0, has_side_effects=True, vmem_limit_bytes=52 * 2**20),
+        )(populations, code)
 
     return jax.shard_map(
         on_device, mesh=mesh,

time: 32.1 us -> 29.7 us (0.925)
  Pallas kernels: 28.2 us -> 26.3 us
  local copies, waits for them, and re-layouts: 3.12 us -> 1.67 us
  other arithmetic: 0 us -> 0.97 us
    pallas_call x1, Pallas kernels: 28.2 us -> 26.3 us  [on_device(): pl.pallas_call(functools.partial(kernel, nx, ny), out_shape=(jax.ShapeDty...]
    unnamed x4 -> x2, local copies, waits for them, and re-layouts: 3.12 us -> 1.67 us
    add x0 -> x1, other arithmetic: none -> 0.96 us  [on_device(): code = jnp.where(labels > 0, 1, 0) + jnp.where(solid, 2, 0)]
where the time goes in v4:
time: 29.7 us; the launch traced here: 29.6 us
  Pallas kernels  26.3 us (89%)
  local copies, waits for them, and re-layouts  1.67 us (6%)
  other arithmetic  0.97 us (3%)
  between operations  0.65 us (2%)
    pallas_call x1, Pallas kernels, on_device(): pl.pallas_call(functools.partial(kernel, nx, ny), out_shape=(jax.ShapeDty...  26.3 us
    unnamed x2, local copies, waits for them, and re-layouts  1.67 us
    add x1, other arithmetic, on_device(): code = jnp.where(labels > 0, 1, 0) + jnp.where(solid, 2, 0)  0.96 us

profile of v4, /device:TPU:0, one launch (start us, length us, event | category | flops | bytes accessed | tf_op | source)
XLA Modules:
  0.0 29.6 jit_solution(5239419855687463286)
XLA Ops:
  0.6 1.0 %select_add_fusion.code_ref = s32[4,32,128]{2,1,0:T(8,128)S(1)} fusion(s32[4,32,128]{2,1,0:T(8,128)} %param.5, s32[4,32,128]{2,1,0:T(8,128)} %param.4, pred[32]{0:T(512)(128)(4,1)S(1)} %get-tuple-element.2, pred[32]{0:T(512)(128)(4,1)S(1)} %get-tuple-element.3), kind=kLoop, calls=%fused_computation | loop fusion | flops 114688 | bytes 196672 | tf_op jit(solution)/shard_map/add | solution.py:404
  1.6 26.3 %shard_map.50 = (f32[19,4,32,128]{3,2,1,0:T(8,128)S(1)}, f32[4,32,128]{2,1,0:T(8,128)S(1)}) custom-call(f32[19,4,32,128]{3,2,1,0:T(8,128)} %pops_hbm.1, s32[4,32,128]{2,1,0:T(8,128)S(1)} %select_add_fusion.code_ref), custom_call_target="tpu_custom_call" | custom-call | tf_op jit(solution)/shard_map/pallas_call | solution.py:405
  27.9 1.0 %copy.7 = f32[19,4,32,128]{3,2,1,0:T(8,128)} copy(f32[19,4,32,128]{3,2,1,0:T(8,128)S(1)} %get-tuple-element.6) | data formatting | bytes 2490368
  28.9 0.6 %copy.8 = f32[4,32,128]{2,1,0:T(8,128)} copy(f32[4,32,128]{2,1,0:T(8,128)S(1)} %get-tuple-element.7) | data formatting | bytes 131072
  (1 shorter events, 0.0 us)

commit v5 on v4

--- a/solution.py
+++ b/solution.py
@@ -127,14 +127,14 @@
 
     def phase_messages(ref, k):
         return [
-            ("x", move(ref, (lx, mid), (0, mid), k, xp, gy), None, None),
-            ("x", move(ref, (1, mid), (lx + 1, mid), k + 1, xm, gy), None, None),
+            ("x+", move(ref, (lx, mid), (0, mid), k, xp, gy), None, None),
+            ("x-", move(ref, (1, mid), (lx + 1, mid), k + 1, xm, gy), None, None),
             ("y", move(ref, (own, last), (own, ghost_low), k + 2, gx, gy + 1), up, down),
             ("y", move(ref, (own, first), (own, ghost_high), k + 3, gx, gy - 1), down, up),
-            ("x", move(ref, (lx, last), (0, ghost_low), k + 4, xp, gy + 1), up, down),
-            ("x", move(ref, (1, last), (lx + 1, ghost_low), k + 5, xm, gy + 1), up, down),
-            ("x", move(ref, (lx, first), (0, ghost_high), k + 6, xp, gy - 1), down, up),
-            ("x", move(ref, (1, first), (lx + 1, ghost_high), k + 7, xm, gy - 1), down, up),
+            ("x+", move(ref, (lx, last), (0, ghost_low), k + 4, xp, gy + 1), up, down),
+            ("x-", move(ref, (1, last), (lx + 1, ghost_low), k + 5, xm, gy + 1), up, down),
+            ("x+", move(ref, (lx, first), (0, ghost_high), k + 6, xp, gy - 1), down, up),
+            ("x-", move(ref, (1, first), (lx + 1, ghost_high), k + 7, xm, gy - 1), down, up),
         ]
 
     def field_messages(ref, rows, k):
@@ -194,15 +194,30 @@
     pm0, fm0 = phase_messages(p0, 0), field_messages(f0, y0, 8)
     pm1, fm1 = phase_messages(p1, 16), field_messages(f1, y1, 24)
 
+    odd = lax.rem(gx, 2)
+
+    def sides(near_first, body, before=None, after=None):
+        def side(n, carry):
+            pick = lax.rem(n + odd + (1 if near_first else 0), 2)
+            for action in (before, body, after):
+                if action is body:
+                    plane = pick * (lx - 1)
+                    lax.fori_loop(
+                        0, rt, lambda t, c: body(plane, pl.multiple_of(t * tr, 8)) or c, 0)
+                elif action is not None:
+                    pl.when(pick == 0)(lambda: action(True))
+                    pl.when(pick == 1)(lambda: action(False))
+            return carry
+
+        lax.fori_loop(0, 2, side, 0)
+
     def loop(kind, body):
-        count = {"edge": 2, "inner": lx - 2, "low": 1, "high": 1}[kind]
+        count = {"edge": 2, "inner": lx - 2}[kind]
 
         def step(t, carry):
             plane, row = t // rt, lax.rem(t, rt)
             if kind == "edge":
                 plane = plane * (lx - 1)
-            elif kind == "high":
-                plane = plane + (lx - 1)
             elif kind == "inner":
                 plane = plane + 1
             body(plane, pl.multiple_of(row * tr, 8))
@@ -323,6 +338,13 @@
         return 2.0 * red / tree(list(f)) - 1.0
 
 
+    def send(ref, messages, low):
+        gather_red(ref, 1 if low else lx, -1 if low else 1)
+        each(messages, "x-" if low else "x+", "start")
+
+    def take(messages, low):
+        each(messages, "x+" if low else "x-", "wait_recv")
+
     def first_plane(x, carry):
         load_plane(x).wait()
 
@@ -335,10 +357,7 @@
 
     lax.fori_loop(0, lx, first_plane, 0)
     each(pm0, None, "wait_recv")
-    for side, x, ex, name in (("high", lx, 1, "x+"), ("low", 1, -1, "x-")):
-        loop(side, functools.partial(colour, f0, p0))
-        gather_red(f0, x, ex)
-        each(fm0, name, "start")
+    sides(False, functools.partial(colour, f0, p0), after=functools.partial(send, f0, fm0))
     loop("inner", functools.partial(colour, f0, p0))
     pack(f0, y0)
     each(fm0, "y", "start")
@@ -351,44 +370,29 @@
         collide(f1, x, r, f)
 
     loop("inner", inner)
-    each(fm0, "x", "wait_recv")
-
     def edge_phase(x, r):
         p1[x + 1, pl.ds(PAD + r, tr)] = mix(f0, x, r, arrive(f0, x, r))
 
-    loop("edge", edge_phase)
-    each(pm1, None, "start")
+    sides(True, edge_phase, before=functools.partial(take, fm0),
+          after=lambda low: each(pm1, "x-" if low else "x+", "start"))
+    each(pm1, "y", "start")
     loop("edge", lambda x, r: collide(f1, x, r, arrive(f0, x, r)))
     each(pm1, None, "wait_recv")
-    for side, x, ex, name in (("high", lx, 1, "x+"), ("low", 1, -1, "x-")):
-        loop(side, functools.partial(colour, f1, p1))
-        gather_red(f1, x, ex)
-        each(fm1, name, "start")
+    sides(False, functools.partial(colour, f1, p1), after=functools.partial(send, f1, fm1))
     loop("inner", functools.partial(colour, f1, p1))
     pack(f1, y1)
     each(fm1, "y", "start")
     each(fm1, "y", "wait_recv")
     unpack(f1, y1)
 
-    def finish(first_x, stride, count):
-        def plane(n, carry):
-            x = first_x + n * stride
-
-            def step(t, carry):
-                r = pl.multiple_of(t * tr, 8)
-                f = arrive(f1, x, r)
-                for i in range(19):
-                    out_ref[i, x, pl.ds(r, tr)] = f[i]
-                phase_ref[x, pl.ds(r, tr)] = mix(f1, x, r, f)
-                return carry
-
-            return lax.fori_loop(0, rt, step, carry)
-
-        lax.fori_loop(0, count, plane, 0)
-
-    finish(1, 1, lx - 2)
-    each(fm1, "x", "wait_recv")
-    finish(0, lx - 1, 2)
+    def finish(x, r):
+        f = arrive(f1, x, r)
+        for i in range(19):
+            out_ref[i, x, pl.ds(r, tr)] = f[i]
+        phase_ref[x, pl.ds(r, tr)] = mix(f1, x, r, f)
+
+    loop("inner", finish)
+    sides(True, finish, before=functools.partial(take, fm1))
     for messages in (pm0, fm0, pm1, fm1):
         each(messages, None, "wait_send")
 

time: 29.7 us -> 29.6 us (level)
  no operation moved by 1% of the time
where the time goes in v5:
time: 29.6 us; the launch traced here: 29.5 us
  Pallas kernels  26.2 us (89%)
  local copies, waits for them, and re-layouts  1.67 us (6%)
  other arithmetic  0.97 us (3%)
  between operations  0.65 us (2%)
    pallas_call x1, Pallas kernels, on_device(): pl.pallas_call(functools.partial(kernel, nx, ny), out_shape=(jax.ShapeDty...  26.2 us
    unnamed x2, local copies, waits for them, and re-layouts  1.67 us
    add x1, other arithmetic, on_device(): code = jnp.where(labels > 0, 1, 0) + jnp.where(solid, 2, 0)  0.96 us

profile of v5, /device:TPU:0, one launch (start us, length us, event | category | flops | bytes accessed | tf_op | source)
XLA Modules:
  0.0 29.5 jit_solution(8532694152647784589)
XLA Ops:
  0.6 1.0 %select_add_fusion.code_ref = s32[4,32,128]{2,1,0:T(8,128)S(1)} fusion(s32[4,32,128]{2,1,0:T(8,128)} %param.5, s32[4,32,128]{2,1,0:T(8,128)} %param.4, pred[32]{0:T(512)(128)(4,1)S(1)} %get-tuple-element.2, pred[32]{0:T(512)(128)(4,1)S(1)} %get-tuple-element.3), kind=kLoop, calls=%fused_computation | loop fusion | flops 114688 | bytes 196672 | tf_op jit(solution)/shard_map/add | solution.py:408
  1.6 26.2 %shard_map.50 = (f32[19,4,32,128]{3,2,1,0:T(8,128)S(1)}, f32[4,32,128]{2,1,0:T(8,128)S(1)}) custom-call(f32[19,4,32,128]{3,2,1,0:T(8,128)} %pops_hbm.1, s32[4,32,128]{2,1,0:T(8,128)S(1)} %select_add_fusion.code_ref), custom_call_target="tpu_custom_call" | custom-call | tf_op jit(solution)/shard_map/pallas_call | solution.py:409
  27.8 1.0 %copy.7 = f32[19,4,32,128]{3,2,1,0:T(8,128)} copy(f32[19,4,32,128]{3,2,1,0:T(8,128)S(1)} %get-tuple-element.6) | data formatting | bytes 2490368
  28.8 0.6 %copy.8 = f32[4,32,128]{2,1,0:T(8,128)} copy(f32[4,32,128]{2,1,0:T(8,128)S(1)} %get-tuple-element.7) | data formatting | bytes 131072
  (1 shorter events, 0.0 us)

commit v6 on v5

--- a/solution.py
+++ b/solution.py
@@ -87,8 +87,7 @@
            f0, f1, p0, p1, rho_ref, pops_ref, y0, y1, load_sem,
            send_sem, recv_sem):
     lx, ly, lz = code_ref.shape
-    tr = 32 if ly % 32 == 0 else 8
-    rt = ly // tr
+    wide, narrow = [next(n for n in (size, 8) if ly % n == 0) for size in (32, 16)]
     top = PAD + ly
     gx, gy = lax.axis_index("gx"), lax.axis_index("gy")
     xp, xm = lax.rem(gx + 1, nx), lax.rem(gx + nx - 1, nx)
@@ -196,14 +195,15 @@
 
     odd = lax.rem(gx, 2)
 
-    def sides(near_first, body, before=None, after=None):
+    def sides(near_first, body, before=None, after=None, tr=wide):
         def side(n, carry):
             pick = lax.rem(n + odd + (1 if near_first else 0), 2)
             for action in (before, body, after):
                 if action is body:
                     plane = pick * (lx - 1)
                     lax.fori_loop(
-                        0, rt, lambda t, c: body(plane, pl.multiple_of(t * tr, 8)) or c, 0)
+                        0, ly // tr,
+                        lambda t, c: body(plane, (pl.multiple_of(t * tr, 8), tr)) or c, 0)
                 elif action is not None:
                     pl.when(pick == 0)(lambda: action(True))
                     pl.when(pick == 1)(lambda: action(False))
@@ -211,7 +211,8 @@
 
         lax.fori_loop(0, 2, side, 0)
 
-    def loop(kind, body):
+    def loop(kind, body, tr=wide):
+        rt = ly // tr
         count = {"edge": 2, "inner": lx - 2}[kind]
 
         def step(t, carry):
@@ -220,7 +221,7 @@
                 plane = plane * (lx - 1)
             elif kind == "inner":
                 plane = plane + 1
-            body(plane, pl.multiple_of(row * tr, 8))
+            body(plane, (pl.multiple_of(row * tr, 8), tr))
             return carry
 
         lax.fori_loop(0, count * rt, step, 0)
@@ -253,18 +254,18 @@
     each(pm0, None, "start")
 
     def solid_at(x, r):
-        return code_ref[x, pl.ds(r, tr)] > 1
+        return code_ref[x, pl.ds(*r)] > 1
 
     def collide(ref, x, r, f):
         solid = solid_at(x, r)
         relaxed, rho = relax(f)
-        rho_ref[x, pl.ds(r, tr)] = rho
+        rho_ref[x, pl.ds(*r)] = rho
         for i in range(19):
-            ref[x + 1, SLOT[i], pl.ds(PAD + r, tr)] = jnp.where(solid, f[OPP[i]], relaxed[i])
+            ref[x + 1, SLOT[i], pl.ds(PAD + r[0], r[1])] = jnp.where(solid, f[OPP[i]], relaxed[i])
 
     def colour(ref, pref, x, r):
-        at = pl.ds(PAD + r, tr)
-        up_r, dn_r = pl.ds(PAD + 1 + r, tr), pl.ds(PAD - 1 + r, tr)
+        at = pl.ds(PAD + r[0], r[1])
+        up_r, dn_r = pl.ds(PAD + 1 + r[0], r[1]), pl.ds(PAD - 1 + r[0], r[1])
         p = pref[x + 1, at]
         e, w = pref[x + 2, at], pref[x, at]
         n, s = pref[x + 1, up_r], pref[x + 1, dn_r]
@@ -285,7 +286,7 @@
         g2 = (xx + yy) + zz
         inv = lax.rsqrt(jnp.maximum(g2, 0.01))
         inv = jnp.where(solid_at(x, r), 0.0, inv)
-        rho = rho_ref[x, pl.ds(r, tr)]
+        rho = rho_ref[x, pl.ds(*r)]
         c18 = (0.1 / 18.0) * inv
         c36 = 0.5 * c18
         k18 = (0.175 / 18.0) * (rho * (1.0 - p * p)) * inv
@@ -323,7 +324,7 @@
             ref[x + 1, SLOT[key], at] = value
 
     def pull(ref, x, r, key, ex, ey):
-        return ref[x + 1 - ex, SLOT[key], pl.ds(PAD - ey + r, tr)]
+        return ref[x + 1 - ex, SLOT[key], pl.ds(PAD - ey + r[0], r[1])]
 
     def arrive(ref, x, r):
         return [pull(ref, x, r, i, e[0], e[1]) for i, e in enumerate(E)]
@@ -349,11 +350,11 @@
         load_plane(x).wait()
 
         def step(t, carry):
-            r = pl.multiple_of(t * tr, 8)
-            collide(f0, x, r, [pops_ref[i, x, pl.ds(r, tr)] for i in range(19)])
+            r = (pl.multiple_of(t * narrow, 8), narrow)
+            collide(f0, x, r, [pops_ref[i, x, pl.ds(*r)] for i in range(19)])
             return carry
 
-        return lax.fori_loop(0, rt, step, carry)
+        return lax.fori_loop(0, ly // narrow, step, carry)
 
     lax.fori_loop(0, lx, first_plane, 0)
     each(pm0, None, "wait_recv")
@@ -366,17 +367,17 @@
 
     def inner(x, r):
         f = arrive(f0, x, r)
-        p1[x + 1, pl.ds(PAD + r, tr)] = mix(f0, x, r, f)
+        p1[x + 1, pl.ds(PAD + r[0], r[1])] = mix(f0, x, r, f)
         collide(f1, x, r, f)
 
-    loop("inner", inner)
+    loop("inner", inner, narrow)
     def edge_phase(x, r):
-        p1[x + 1, pl.ds(PAD + r, tr)] = mix(f0, x, r, arrive(f0, x, r))
+        p1[x + 1, pl.ds(PAD + r[0], r[1])] = mix(f0, x, r, arrive(f0, x, r))
 
     sides(True, edge_phase, before=functools.partial(take, fm0),
           after=lambda low: each(pm1, "x-" if low else "x+", "start"))
     each(pm1, "y", "start")
-    loop("edge", lambda x, r: collide(f1, x, r, arrive(f0, x, r)))
+    loop("edge", lambda x, r: collide(f1, x, r, arrive(f0, x, r)), narrow)
     each(pm1, None, "wait_recv")
     sides(False, functools.partial(colour, f1, p1), after=functools.partial(send, f1, fm1))
     loop("inner", functools.partial(colour, f1, p1))
@@ -388,8 +389,8 @@
     def finish(x, r):
         f = arrive(f1, x, r)
         for i in range(19):
-            out_ref[i, x, pl.ds(r, tr)] = f[i]
-        phase_ref[x, pl.ds(r, tr)] = mix(f1, x, r, f)
+            out_ref[i, x, pl.ds(*r)] = f[i]
+        phase_ref[x, pl.ds(*r)] = mix(f1, x, r, f)
 
     loop("inner", finish)
     sides(True, finish, before=functools.partial(take, fm1))

time: 29.6 us -> 29.6 us (level)
  no operation moved by 1% of the time
where the time goes in v6:
time: 29.6 us; the launch traced here: 29.5 us
  Pallas kernels  26.2 us (89%)
  local copies, waits for them, and re-layouts  1.67 us (6%)
  other arithmetic  0.97 us (3%)
  between operations  0.65 us (2%)
    pallas_call x1, Pallas kernels, on_device(): pl.pallas_call(functools.partial(kernel, nx, ny), out_shape=(jax.ShapeDty...  26.2 us
    unnamed x2, local copies, waits for them, and re-layouts  1.67 us
    add x1, other arithmetic, on_device(): code = jnp.where(labels > 0, 1, 0) + jnp.where(solid, 2, 0)  0.96 us

profile of v6, /device:TPU:0, one launch (start us, length us, event | category | flops | bytes accessed | tf_op | source)
XLA Modules:
  0.0 29.5 jit_solution(17647893152499098936)
XLA Ops:
  0.6 1.0 %select_add_fusion.code_ref = s32[4,32,128]{2,1,0:T(8,128)S(1)} fusion(s32[4,32,128]{2,1,0:T(8,128)} %param.5, s32[4,32,128]{2,1,0:T(8,128)} %param.4, pred[32]{0:T(512)(128)(4,1)S(1)} %get-tuple-element.2, pred[32]{0:T(512)(128)(4,1)S(1)} %get-tuple-element.3), kind=kLoop, calls=%fused_computation | loop fusion | flops 114688 | bytes 196672 | tf_op jit(solution)/shard_map/add | solution.py:409
  1.6 26.2 %shard_map.50 = (f32[19,4,32,128]{3,2,1,0:T(8,128)S(1)}, f32[4,32,128]{2,1,0:T(8,128)S(1)}) custom-call(f32[19,4,32,128]{3,2,1,0:T(8,128)} %pops_hbm.1, s32[4,32,128]{2,1,0:T(8,128)S(1)} %select_add_fusion.code_ref), custom_call_target="tpu_custom_call" | custom-call | tf_op jit(solution)/shard_map/pallas_call | solution.py:410
  27.8 1.0 %copy.7 = f32[19,4,32,128]{3,2,1,0:T(8,128)} copy(f32[19,4,32,128]{3,2,1,0:T(8,128)S(1)} %get-tuple-element.6) | data formatting | bytes 2490368
  28.8 0.6 %copy.8 = f32[4,32,128]{2,1,0:T(8,128)} copy(f32[4,32,128]{2,1,0:T(8,128)S(1)} %get-tuple-element.7) | data formatting | bytes 131072
  (1 shorter events, 0.0 us)

commit v7 on v6

--- a/solution.py
+++ b/solution.py
@@ -226,6 +226,17 @@
 
         lax.fori_loop(0, count * rt, step, 0)
 
+    def middle(body):
+        if ly > 16:
+            lax.fori_loop(1, lx - 1, lambda x, c: body(x, (8, ly - 16)) or c, 0)
+
+    def border(body):
+        def step(t, carry):
+            body(1 + t // 2, (pl.multiple_of(lax.rem(t, 2) * (ly - 8), 8), 8))
+            return carry
+
+        lax.fori_loop(0, 2 * (lx - 2), step, 0)
+
     zero = jnp.zeros((8, lz), jnp.float32)
 
     def fill(x, carry):
@@ -362,15 +373,17 @@
     loop("inner", functools.partial(colour, f0, p0))
     pack(f0, y0)
     each(fm0, "y", "start")
-    each(fm0, "y", "wait_recv")
-    unpack(f0, y0)
 
     def inner(x, r):
         f = arrive(f0, x, r)
         p1[x + 1, pl.ds(PAD + r[0], r[1])] = mix(f0, x, r, f)
         collide(f1, x, r, f)
 
-    loop("inner", inner, narrow)
+    middle(inner)
+    each(fm0, "y", "wait_recv")
+    unpack(f0, y0)
+    border(inner)
+
     def edge_phase(x, r):
         p1[x + 1, pl.ds(PAD + r[0], r[1])] = mix(f0, x, r, arrive(f0, x, r))
 
@@ -383,8 +396,6 @@
     loop("inner", functools.partial(colour, f1, p1))
     pack(f1, y1)
     each(fm1, "y", "start")
-    each(fm1, "y", "wait_recv")
-    unpack(f1, y1)
 
     def finish(x, r):
         f = arrive(f1, x, r)
@@ -392,7 +403,11 @@
             out_ref[i, x, pl.ds(*r)] = f[i]
         phase_ref[x, pl.ds(*r)] = mix(f1, x, r, f)
 
-    loop("inner", finish)
+    middle(finish)
+    each(fm1, "y", "wait_recv")
+    unpack(f1, y1)
+    border(finish)
+
     sides(True, finish, before=functools.partial(take, fm1))
     for messages in (pm0, fm0, pm1, fm1):
         each(messages, None, "wait_send")

time: 29.6 us -> 29.6 us (level)
  no operation moved by 1% of the time
where the time goes in v7:
time: 29.6 us; the launch traced here: 29.5 us
  Pallas kernels  26.2 us (89%)
  local copies, waits for them, and re-layouts  1.67 us (6%)
  other arithmetic  0.97 us (3%)
  between operations  0.65 us (2%)
    pallas_call x1, Pallas kernels, on_device(): pl.pallas_call(functools.partial(kernel, nx, ny), out_shape=(jax.ShapeDty...  26.2 us
    unnamed x2, local copies, waits for them, and re-layouts  1.67 us
    add x1, other arithmetic, on_device(): code = jnp.where(labels > 0, 1, 0) + jnp.where(solid, 2, 0)  0.96 us

profile of v7, /device:TPU:0, one launch (start us, length us, event | category | flops | bytes accessed | tf_op | source)
XLA Modules:
  0.0 29.5 jit_solution(9177770390145660748)
XLA Ops:
  0.6 1.0 %select_add_fusion.code_ref = s32[4,32,128]{2,1,0:T(8,128)S(1)} fusion(s32[4,32,128]{2,1,0:T(8,128)} %param.5, s32[4,32,128]{2,1,0:T(8,128)} %param.4, pred[32]{0:T(512)(128)(4,1)S(1)} %get-tuple-element.2, pred[32]{0:T(512)(128)(4,1)S(1)} %get-tuple-element.3), kind=kLoop, calls=%fused_computation | loop fusion | flops 114688 | bytes 196672 | tf_op jit(solution)/shard_map/add | solution.py:424
  1.6 26.2 %shard_map.50 = (f32[19,4,32,128]{3,2,1,0:T(8,128)S(1)}, f32[4,32,128]{2,1,0:T(8,128)S(1)}) custom-call(f32[19,4,32,128]{3,2,1,0:T(8,128)} %pops_hbm.1, s32[4,32,128]{2,1,0:T(8,128)S(1)} %select_add_fusion.code_ref), custom_call_target="tpu_custom_call" | custom-call | tf_op jit(solution)/shard_map/pallas_call | solution.py:425
  27.8 1.0 %copy.7 = f32[19,4,32,128]{3,2,1,0:T(8,128)} copy(f32[19,4,32,128]{3,2,1,0:T(8,128)S(1)} %get-tuple-element.6) | data formatting | bytes 2490368
  28.8 0.6 %copy.8 = f32[4,32,128]{2,1,0:T(8,128)} copy(f32[4,32,128]{2,1,0:T(8,128)S(1)} %get-tuple-element.7) | data formatting | bytes 131072
  (1 shorter events, 0.0 us)
